TPU v7x, 256 devices: a whole 4x4x8 slice. The times are simulated.
256 devices in a mesh: grp: 8 (over x, z_hi), mem: 32 (over y, z_lo, core).
Axes of the slice: x: 4, y: 4, z: 8 (z_hi: 2, z_lo: 4; z = z_hi * 4 + z_lo), core: 2. Of those that a mesh axis runs over, the one named last changes fastest.
Arguments:
- initial_state: bfloat16 [128, 128, 64, 2, 128], P('grp', 'mem'), may hold values from -6 to 6
- cotangent: bfloat16 [128, 128, 64, 2, 128], P('grp', 'mem'), may hold values from -6 to 6
- gate_bank: bfloat16 [3, 4, 2, 128, 128], replicated, may hold values from -0.375 to 0.375
- slice_index: int32 [3], replicated, may hold values from 0 to 3
- mode_order: int32 [3, 7], replicated, may hold values from 0 to 6, each once within a row
Outputs:
- gate_grads: float32 [3, 2, 128, 128], replicated
- state_grad: bfloat16 [128, 128, 64, 2, 128], P('grp', None, 'mem')
Inputs may be any that keep to these rules, and one draw needn't show every extreme that they name: `mode_order`: each row names every position 0 to 6 once.
All inputs are finite; a program needn't handle non-finite values.
Results may differ from a plain program's by a relative error of at most 0.0057.
Values may be sent and summed in bfloat16 or wider, within the bound.
A program may use at most 64 MiB of HBM per device.

v0:
```python
import jax
import jax.numpy as jnp
from jax import lax
from jax.sharding import PartitionSpec as P


def index_table(order_row, width):
    places_count = order_row.shape[0]
    states = jnp.arange(width, dtype=jnp.int32)
    places = jnp.arange(places_count, dtype=jnp.int32)
    bits = states[:, None] >> places[None, :] & 1
    mapped = jnp.sum(bits << order_row[None, :], axis=1)
    return (mapped[:, None] == states[None, :]).astype(jnp.float32)


def gate_matrix(gate_bank, slice_index, mode_order, number):
    width = gate_bank.shape[-1]
    chosen = lax.dynamic_index_in_dim(
        gate_bank[number], slice_index[number], 0, keepdims=False
    ).astype(jnp.float32)
    picker = index_table(mode_order[number], width)
    moved = jnp.matmul(
        jnp.matmul(picker, chosen, precision=lax.Precision.HIGHEST),
        picker.T,
        precision=lax.Precision.HIGHEST,
    )
    upper = jnp.stack([moved[0], -moved[1]], axis=1)
    lower = jnp.stack([moved[1], moved[0]], axis=1)
    return (jnp.stack([upper, lower], axis=0).astype(jnp.bfloat16), picker)


def contract(form, left, right):
    return jnp.einsum(form, left, right, preferred_element_type=jnp.float32)


def fold_planes(grad_real):
    return jnp.stack(
        [
            grad_real[0, :, 0, :] + grad_real[1, :, 1, :],
            grad_real[1, :, 0, :] - grad_real[0, :, 1, :],
        ]
    )


def local(initial_state, cotangent, gate_bank, slice_index, mode_order):
    width = gate_bank.shape[-1]
    remaining = initial_state.shape[2]
    mats = [gate_matrix(gate_bank, slice_index, mode_order, number) for number in range(3)]
    first = mats[0][0]
    second = mats[1][0]
    third = mats[2][0]
    layer_start = contract("nmrdj,cidj->nmrci", initial_state, first).astype(jnp.bfloat16)
    arrived = lax.all_to_all(layer_start, "mem", split_axis=2, concat_axis=1, tiled=True)
    layer_two = contract("njrdk,cidj->nirck", arrived, second).astype(jnp.bfloat16)
    last_state = lax.all_to_all(layer_two, "grp", split_axis=1, concat_axis=0, tiled=True)
    cot_last = lax.all_to_all(
        lax.all_to_all(cotangent, "mem", split_axis=2, concat_axis=1, tiled=True),
        "grp",
        split_axis=1,
        concat_axis=0,
        tiled=True,
    )
    back_two = contract("imrck,cidj->jmrdk", cot_last, third).astype(jnp.bfloat16)
    grad_three = fold_planes(contract("imrck,jmrdk->cidj", cot_last, last_state))
    back_middle = lax.all_to_all(back_two, "grp", split_axis=0, concat_axis=1, tiled=True)
    grad_two = fold_planes(contract("nirck,njrdk->cidj", back_middle, arrived))
    back_one = contract("nirck,cidj->njrdk", back_middle, second).astype(jnp.bfloat16)
    state_grad = contract("nmrci,cidj->nmrdj", back_one, first).astype(jnp.bfloat16)
    back_first = lax.all_to_all(back_one, "mem", split_axis=1, concat_axis=2, tiled=True)
    grad_one = fold_planes(contract("nmrci,nmrdj->cidj", back_first, initial_state))
    totals = lax.psum((grad_one, grad_two, grad_three), ("grp", "mem"))
    factor = 1.0 / (width * remaining**0.5)
    grads = []
    for number in range(3):
        picker = mats[number][1]
        restored = jnp.matmul(
            jnp.matmul(picker.T, totals[number], precision=lax.Precision.HIGHEST),
            picker,
            precision=lax.Precision.HIGHEST,
        )
        grads.append(restored * factor)
    return (jnp.stack(grads), state_grad)


def solution(mesh):
    in_specs = (P("grp", "mem", None, None, None), P("grp", "mem", None, None, None), P(), P(), P())
    out_specs = (P(), P("grp", None, "mem", None, None))
    return jax.shard_map(local, mesh=mesh, in_specs=in_specs, out_specs=out_specs, check_vma=False)
```

profile of v0, /device:TPU:1, one launch (start us, length us, event | category | flops | bytes accessed | tf_op | source)
XLA Modules:
  0.0 614.1 jit_solution(7340419677188737218)
XLA Ops:
  7.2 4.0 copy.104
  11.2 60.3 %all_to_all.108 = bf16[16,4,64,2,128]{4,0,3,1,2:T(8,128)(2,1)S(1)} all-to-all(bf16[16,4,64,2,128]{4,0,3,1,2:T(8,128)(2,1)S(1)} %copy.104), channel_id=1, replica_groups=mesh['grp'=8,'mem'=32] {'mem'}, dimensions={2} | all-to-all | bytes 4194304 | tf_op jit(solution)/shard_map/all_to_all | solution.py:57
  71.5 1.9 copy.106
  73.5 8.1 %all-to-all-start.1 = ((bf16[16,128,2,2,128]{4,0,3,2,1:T(8,128)(2,1)}), bf16[16,128,2,2,128]{4,0,3,2,1:T(8,128)(2,1)S(1)}, u32[]{:S(2)}, u32[]{:S(2)}) async-start(bf16[16,128,2,2,128]{4,0,3,2,1:T(8,128)(2,1)} %bitcast.278), calls=%async_computation.1 | async-start | bytes 4194304 | tf_op jit(solution)/shard_map/all_to_all | solution.py:56
  84.9 0.8 copy-done.6
  86.4 2.9 copy.118
  89.4 42.6 %all-to-all-done.1 = bf16[16,128,2,2,128]{4,0,3,2,1:T(8,128)(2,1)S(1)} async-done(((bf16[16,128,2,2,128]{4,0,3,2,1:T(8,128)(2,1)}), bf16[16,128,2,2,128]{4,0,3,2,1:T(8,128)(2,1)S(1)}, u32[]{:S(2)}, u32[]{:S(2)}) %all-to-all-start.1) | async-done | bytes 2097184 | tf_op jit(solution)/shard_map/all_to_all | solution.py:56
  132.0 5.8 all-to-all-start.4
  140.9 1.3 copy-done.2
  143.0 3.5 copy.110
  146.5 41.2 %all-to-all-done.4 = bf16[16,4,64,2,128]{4,1,0,3,2:T(4,128)(2,1)} async-done(((bf16[16,4,64,2,128]{4,1,0,3,2:T(4,128)(2,1)}), bf16[16,4,64,2,128]{4,1,0,3,2:T(4,128)(2,1)}, u32[]{:S(2)}, u32[]{:S(2)}) %all-to-all-start.4) | async-done | bytes 2097184 | tf_op jit(solution)/shard_map/all_to_all | solution.py:53
  187.7 5.0 all-to-all-start.2
  195.1 2.7 copy.119
  197.9 1.3 copy-done.4
  199.9 3.5 copy.126
  203.4 38.6 %all-to-all-done.2 = bf16[128,16,2,2,128]{4,2,1,3,0:T(2,128)(2,1)S(1)} async-done(((bf16[128,16,2,2,128]{4,2,1,3,0:T(2,128)(2,1)}), bf16[128,16,2,2,128]{4,2,1,3,0:T(2,128)(2,1)S(1)}, u32[]{:S(2)}, u32[]{:S(2)}) %all-to-all-start.2) | async-done | bytes 2097184 | tf_op jit(solution)/shard_map/all_to_all | solution.py:65
  242.0 5.3 all-to-all-start.5
  247.9 0.7 bitcast_convert_fusion.3
  248.6 1.3 copy-done
  250.0 3.6 copy.113
  253.5 38.0 %all-to-all-done.5 = bf16[16,128,2,2,128]{4,2,0,3,1:T(2,128)(2,1)} async-done(((bf16[16,128,2,2,128]{4,2,0,3,1:T(2,128)(2,1)}), bf16[16,128,2,2,128]{4,2,0,3,1:T(2,128)(2,1)}, u32[]{:S(2)}, u32[]{:S(2)}) %all-to-all-start.5) | async-done | bytes 2097184 | tf_op jit(solution)/shard_map/all_to_all | solution.py:55
  291.6 11.0 %all-to-all-start.3 = ((bf16[16,128,2,2,128]{4,2,0,3,1:T(2,128)(2,1)}), bf16[16,128,2,2,128]{4,2,0,3,1:T(2,128)(2,1)}, u32[]{:S(2)}, u32[]{:S(2)}) async-start(bf16[16,128,2,2,128]{4,2,0,3,1:T(2,128)(2,1)} %copy.113), calls=%async_computation.3 | async-start | bytes 4194304 | tf_op jit(solution)/shard_map/all_to_all | solution.py:69
  302.8 2.3 copy.127
  307.1 1.1 copy-done.5
  309.6 42.8 %all-to-all-done.3 = bf16[16,128,2,2,128]{4,2,0,3,1:T(2,128)(2,1)} async-done(((bf16[16,128,2,2,128]{4,2,0,3,1:T(2,128)(2,1)}), bf16[16,128,2,2,128]{4,2,0,3,1:T(2,128)(2,1)}, u32[]{:S(2)}, u32[]{:S(2)}) %all-to-all-start.3) | async-done | bytes 2097184 | tf_op jit(solution)/shard_map/all_to_all | solution.py:69
  352.4 4.1 copy.114
  358.8 3.5 copy.135
  362.3 239.7 %all-reduce.3.cloned.1.call-done = (f32[2,128,128]{1,2,0:T(8,128)}, f32[2,128,128]{1,2,0:T(8,128)}, f32[2,128,128]{2,1,0:T(8,128)}) async-done(((f32[2,128,128]{1,2,0:T(8,128)}, f32[2,128,128]{1,2,0:T(8,128)}, f32[2,128,128]{2,1,0:T(8,128)}), (f32[2,128,128]{1,2,0:T(8,128)}, f32[2,128,128]{1,2,0:T(8,128)}, f32[2,128,128]{2,1,0:T(8,128)})) %all-reduce.3.cloned.1.call-update) | async-done | bytes 393232 | tf_op jit(solution)/shard_map/psum | solution.py:71
  601.9 1.2 convolution_bitcast_fusion.1
  603.5 1.2 convolution_bitcast_fusion.2
  605.0 1.2 convolution_bitcast_fusion.3
  606.5 0.8 pad_maximum_fusion
  (60 shorter events, 12.5 us)
Async XLA Ops:
  73.5 8.1 %copy-start.9 = (s32[3]{0:T(128)S(1)}, s32[3]{0:T(128)}, u32[]{:S(2)}) copy-start(s32[3]{0:T(128)} %param.8) | copy-start | bytes 40
  73.5 10.6 %copy-start.10 = (s32[3,7]{1,0:T(4,128)S(1)}, s32[3,7]{1,0:T(4,128)}, u32[]{:S(2)}) copy-start(s32[3,7]{1,0:T(4,128)} %param.9) | copy-start | bytes 256
  73.5 10.7 %copy-start.8 = (bf16[3,4,2,128,128]{4,3,2,1,0:T(8,128)(2,1)S(1)}, bf16[3,4,2,128,128]{4,3,2,1,0:T(8,128)(2,1)}, u32[]{:S(2)}) copy-start(bf16[3,4,2,128,128]{4,3,2,1,0:T(8,128)(2,1)} %param.7) | copy-start | bytes 2359300
  73.5 58.5 %all-to-all-start.1 = ((bf16[16,128,2,2,128]{4,0,3,2,1:T(8,128)(2,1)}), bf16[16,128,2,2,128]{4,0,3,2,1:T(8,128)(2,1)S(1)}, u32[]{:S(2)}, u32[]{:S(2)}) async-start(bf16[16,128,2,2,128]{4,0,3,2,1:T(8,128)(2,1)} %bitcast.278), calls=%async_computation.1 | async-start | bytes 4194304 | tf_op jit(solution)/shard_map/all_to_all | solution.py:56
  84.1 1.6 copy-start.6
  132.0 55.7 %all-to-all-start.4 = ((bf16[16,4,64,2,128]{4,1,0,3,2:T(4,128)(2,1)}), bf16[16,4,64,2,128]{4,1,0,3,2:T(4,128)(2,1)}, u32[]{:S(2)}, u32[]{:S(2)}) async-start(bf16[16,4,64,2,128]{4,1,0,3,2:T(4,128)(2,1)} %copy.118), calls=%async_computation.4 | async-start | bytes 4194304 | tf_op jit(solution)/shard_map/all_to_all | solution.py:53
  140.9 1.3 copy-start.2
  187.7 54.3 %all-to-all-start.2 = ((bf16[128,16,2,2,128]{4,2,1,3,0:T(2,128)(2,1)}), bf16[128,16,2,2,128]{4,2,1,3,0:T(2,128)(2,1)S(1)}, u32[]{:S(2)}, u32[]{:S(2)}) async-start(bf16[128,16,2,2,128]{4,2,1,3,0:T(2,128)(2,1)} %copy.110), calls=%async_computation.2 | async-start | bytes 4194304 | tf_op jit(solution)/shard_map/all_to_all | solution.py:65
  197.9 1.4 copy-start.4
  242.0 49.6 %all-to-all-start.5 = ((bf16[16,128,2,2,128]{4,2,0,3,1:T(2,128)(2,1)}), bf16[16,128,2,2,128]{4,2,0,3,1:T(2,128)(2,1)}, u32[]{:S(2)}, u32[]{:S(2)}) async-start(bf16[16,128,2,2,128]{4,2,0,3,1:T(2,128)(2,1)} %copy.126), calls=%async_computation.5 | async-start | bytes 4194304 | tf_op jit(solution)/shard_map/all_to_all | solution.py:55
  248.6 1.3 copy-start
  291.6 60.8 %all-to-all-start.3 = ((bf16[16,128,2,2,128]{4,2,0,3,1:T(2,128)(2,1)}), bf16[16,128,2,2,128]{4,2,0,3,1:T(2,128)(2,1)}, u32[]{:S(2)}, u32[]{:S(2)}) async-start(bf16[16,128,2,2,128]{4,2,0,3,1:T(2,128)(2,1)} %copy.113), calls=%async_computation.3 | async-start | bytes 4194304 | tf_op jit(solution)/shard_map/all_to_all | solution.py:69
  302.5 299.4 %all-reduce.3.cloned.1.call-start = ((), (), s32[]{:S(2)}) async-start(), calls=%async_computation.6 | async-start | bytes 786432 | tf_op jit(solution)/shard_map/psum | solution.py:71
  302.8 2.3 copy-start.3
  306.6 1.6 copy-start.5
  352.4 4.1 copy-start.7
  356.5 1.6 copy-start.1
Sparse Core Ops, SparseCore 0:
  358.1 243.8 all-reduce.2
where the time goes:
time: 615 us; the launch traced here: 614 us
  waiting for transfers between devices  443 us (72%)
  blocking collectives  60.3 us (10%)
  local copies, waits for them, and re-layouts  40.4 us (7%)
  starting transfers between devices  35.4 us (6%)
  between operations  20.2 us (3%)
  matrix products  11.9 us (2%)
    psum x1, waiting for transfers between devices, local(): totals = lax.psum((grad_one, grad_two, grad_three), ('grp', 'mem'))  240 us
    all_to_all x1, blocking collectives, local(): lax.all_to_all(cotangent, 'mem', split_axis=2, concat_axis=1, tiled=True)  60.3 us
    all_to_all x1, waiting for transfers between devices, local(): lax.all_to_all(back_one, 'mem', split_axis=1, concat_axis=2, tiled=True)  42.8 us
    all_to_all x1, waiting for transfers between devices, local(): lax.all_to_all(lax.all_to_all(cotangent, 'mem', split_axis=2, concat_axis...  42.6 us
    all_to_all x1, waiting for transfers between devices, local(): lax.all_to_all(layer_start, 'mem', split_axis=2, concat_axis=1, tiled=True)  41.2 us
    all_to_all x1, waiting for transfers between devices, local(): lax.all_to_all(back_two, 'grp', split_axis=0, concat_axis=1, tiled=True)  38.6 us
    all_to_all x1, waiting for transfers between devices, local(): lax.all_to_all(layer_two, 'grp', split_axis=1, concat_axis=0, tiled=True)  38 us
    unnamed x24, local copies, waits for them, and re-layouts  13.5 us
  transfers between devices with their start and end apart: 6, of which 6 were waited for; matrix products, arithmetic and copies ran while one was open for 5% of the time, Pallas kernels for 0%

commit v1 on v0

v1 whole, which is shorter than its diff:
```python
import numpy as np
import jax
import jax.numpy as jnp
from jax import lax
from jax.experimental import pallas as pl
from jax.experimental.pallas import tpu as pltpu
from jax.sharding import PartitionSpec as P

MESH = pl.DeviceIdType.MESH
BF = jnp.bfloat16
F32 = jnp.float32
HIGH = lax.Precision.HIGHEST
NX, NY, NZ, NC = 4, 4, 8, 2
Z_ORDER = (4, 3, 5, 2, 6, 1, 7, 0)


def block_turn():
    mat = np.zeros((256, 256), np.float32)
    for a in range(16):
        for b in range(16):
            mat[b * 16 + a, a * 16 + b] = 1.0
    return mat


def stored_order():
    order = np.zeros(128, np.int32)
    for y in range(4):
        for c in range(2):
            for zl in range(4):
                for ml in range(4):
                    order[y * 32 + c * 16 + zl * 4 + ml] = ((y * 4 + zl) * 2 + c) * 4 + ml
    return order


def output_turn():
    order = stored_order()
    mat = np.zeros((256, 256), np.float32)
    for s in range(64):
        for rc in range(4):
            mat[order[s] * 4 + rc, rc * 64 + s] = 1.0
    return mat


def index_table(order_row, width):
    places_count = order_row.shape[0]
    states = jnp.arange(width, dtype=jnp.int32)
    places = jnp.arange(places_count, dtype=jnp.int32)
    bits = states[:, None] >> places[None, :] & 1
    mapped = jnp.sum(bits << order_row[None, :], axis=1)
    return (mapped[:, None] == states[None, :]).astype(F32)


def gate_matrix(gate_bank, slice_index, mode_order, number):
    width = gate_bank.shape[-1]
    chosen = lax.dynamic_index_in_dim(gate_bank[number], slice_index[number], 0, keepdims=False)
    picker = index_table(mode_order[number], width)
    small = picker.astype(BF)
    moved = jnp.einsum("ia,qab,jb->qij", small, chosen, small, preferred_element_type=F32).astype(BF)
    upper = jnp.stack([moved[0], -moved[1]], axis=1)
    lower = jnp.stack([moved[1], moved[0]], axis=1)
    return jnp.stack([upper, lower], axis=0), picker


def dot(a, b):
    return jnp.dot(a, b, preferred_element_type=F32)


def dot_nt(a, b):
    return lax.dot_general(a, b, (((1,), (1,)), ((), ())), preferred_element_type=F32)


def dot_tn(a, b):
    return lax.dot_general(a, b, (((0,), (0,)), ((), ())), preferred_element_type=F32)


def planes_down(a, b):
    top = jnp.concatenate([a[:, :128], b[:, :128]], axis=1)
    low = jnp.concatenate([a[:, 128:], b[:, 128:]], axis=1)
    return jnp.concatenate([top, low], axis=0)


def planes_up(o, which):
    half = o.shape[0] // 2
    lanes = slice(128 * which, 128 * which + 128)
    return jnp.concatenate([o[:half, lanes], o[half:, lanes]], axis=1)


def with_turned(l):
    return jnp.concatenate([l, jnp.concatenate([-l[:, 128:], l[:, :128]], axis=1)], axis=0)


def kernel(
    craw, xraw, w1f, w1b, w2f, w2b, w3b, turn, outturn, pickers,
    out, eout,
    csend, xsend, call, xq, b2, b2t, b1t, sg, xt, l1t, l2t, sgr, v1acc, e, rx, ryc, rz, fin,
    c_ss, c_rs, x_ss, x_rs, loc, g_ss, g_rs, f_ss, f_rs, s_ss, s_rs,
    e1s, e1r, e2s, e2r, e3s, e3r, e4s, e4r, e5s, e5r,
):
    grp, mem = lax.axis_index("grp"), lax.axis_index("mem")
    x, zh = grp // 2, grp % 2
    y, zl, c = mem // 8, (mem // 2) % 4, mem % 2
    z = zh * 4 + zl

    def device(dx, dy, dz, dc):
        x2, y2, z2, c2 = (x + dx) % NX, (y + dy) % NY, (z + dz) % NZ, (c + dc) % NC
        return (x2 * 2 + z2 // 4, (y2 * 4 + z2 % 4) * 2 + c2)

    def yzc(t):
        return t // 16, t % 8, (t // 8) % 2

    bar = pltpu.get_barrier_semaphore()

    def greet(t, carry):
        dy, dz, dc = yzc(t)
        pl.semaphore_signal(bar, inc=1, device_id=device(0, dy, dz, dc), device_id_type=MESH)
        return carry

    lax.fori_loop(1, 64, greet, 0)
    for dx in range(1, NX):
        pl.semaphore_signal(bar, inc=1, device_id=device(dx, 0, 0, 0), device_id_type=MESH)

    def extract(raw, send):
        def body(i, carry):
            mp, rb = i // 8, i % 8
            rows = pl.ds(pl.multiple_of(16 * rb, 16), 16)
            a = raw[:, 2 * mp, rows, :].reshape(256, 128)
            b = raw[:, 2 * mp + 1, rows, :].reshape(256, 128)
            o = dot(turn[...], jnp.concatenate([a, b], axis=1)).astype(BF)
            for mm in range(2):
                for r in range(8):
                    for cc in range(2):
                        q = (r * 2 + cc) * 16
                        send[8 * rb + r, 2 * mp + mm, :, cc * 128:cc * 128 + 128] = o[q:q + 16, mm * 128:mm * 128 + 128]
            return carry

        lax.fori_loop(0, 16, body, 0)

    extract(craw, csend)
    pl.semaphore_wait(bar, 66)

    m_own = pl.multiple_of(y * 32 + c * 16 + zl * 4, 4)
    n_own = pl.multiple_of(32 * x + 16 * zh, 16)
    nq_own = pl.multiple_of(16 * zh, 16)

    def part_of(dy, dz, dc):
        s = (z + dz + 6) % NZ
        return 2 * ((((y + dy) % NY) * 4 + s % 4) * 2 + (c + dc) % NC) + s // 4

    def c_copy(t):
        dy, dz, dc = yzc(t)
        return pltpu.make_async_remote_copy(
            src_ref=csend.at[part_of(dy, dz, dc)],
            dst_ref=call.at[pl.ds(m_own, 4), pl.ds(n_own, 16), :],
            send_sem=c_ss.at[t], recv_sem=c_rs.at[t],
            device_id=device(0, dy, dz, dc), device_id_type=MESH)

    def x_copy(t):
        dy, dz, dc = yzc(t)
        return pltpu.make_async_remote_copy(
            src_ref=xsend.at[part_of(dy, dz, dc)],
            dst_ref=xq.at[pl.ds(m_own, 4), pl.ds(nq_own, 16), :],
            send_sem=x_ss.at[t], recv_sem=x_rs.at[t],
            device_id=device(0, dy, dz, dc), device_id_type=MESH)

    own_c = pltpu.make_async_copy(csend.at[part_of(0, 0, 0)], call.at[pl.ds(m_own, 4), pl.ds(n_own, 16), :], loc.at[0])
    own_x = pltpu.make_async_copy(xsend.at[part_of(0, 0, 0)], xq.at[pl.ds(m_own, 4), pl.ds(nq_own, 16), :], loc.at[1])

    def start_group(copy, g):
        for dz in Z_ORDER:
            if dz == 0:
                @pl.when(g > 0)
                def _():
                    copy(g * 8).start()
            else:
                copy(g * 8 + dz).start()

    def c_start(g, carry):
        start_group(c_copy, g)
        return carry

    own_c.start()
    lax.fori_loop(0, 8, c_start, 0)
    extract(xraw, xsend)
    own_x.start()

    def m_of(g):
        dy, dc = g // 2, g % 2
        return pl.multiple_of(((y + NY - dy) % NY) * 32 + ((c + NC - dc) % NC) * 16, 16)

    def near(g, way):
        part = call.at[pl.ds(m_of(g), 16), pl.ds(pl.multiple_of(32 * x, 32), 32), :]
        return pltpu.make_async_remote_copy(
            src_ref=part, dst_ref=part, send_sem=g_ss.at[way, g], recv_sem=g_rs.at[way, g],
            device_id=device(1 if way == 0 else NX - 1, 0, 0, 0), device_id_type=MESH)

    def far(g, way):
        owner = (x + NX - 1) % NX if way == 0 else (x + 1) % NX
        part = call.at[pl.ds(m_of(g) + 8 * way, 8), pl.ds(pl.multiple_of(32 * owner, 32), 32), :]
        return pltpu.make_async_remote_copy(
            src_ref=part, dst_ref=part, send_sem=f_ss.at[way, g], recv_sem=f_rs.at[way, g],
            device_id=device(1 if way == 0 else NX - 1, 0, 0, 0), device_id_type=MESH)

    def relay(g):
        for way in range(2):
            near(g, way).wait_recv()
            far(g, way).start()

    def arrive(g, carry):
        for dz in Z_ORDER:
            if dz == 0:
                @pl.when(g > 0)
                def _():
                    c_copy(g * 8).wait_recv()
            else:
                c_copy(g * 8 + dz).wait_recv()

        @pl.when(g == 0)
        def _():
            own_c.wait()

        near(g, 0).start()
        near(g, 1).start()

        @pl.when(g >= 4)
        def _():
            start_group(x_copy, (g - 4) * 2)
            start_group(x_copy, (g - 4) * 2 + 1)

        @pl.when(g >= 1)
        def _():
            relay(g - 1)

        return carry

    lax.fori_loop(0, 8, arrive, 0)
    relay(7)

    def third(g, carry):
        far(g, 0).wait_recv()
        far(g, 1).wait_recv()
        base = m_of(g)
        for p in range(8):
            m = base + 2 * p
            o = dot(w3b[...], planes_down(call[m], call[m + 1])).astype(BF)
            b2[m] = planes_up(o, 0)
            b2[m + 1] = planes_up(o, 1)
        return carry

    lax.fori_loop(0, 8, third, 0)

    def turn_block(src, dst, half, i, to_rows):
        at = pl.ds(pl.multiple_of(16 * i, 16), 16)
        cols = slice(16 * half, 16 * half + 16)
        if to_rows:
            blk = src[at, cols, :]
        else:
            blk = src[cols, at, :]
        o = dot(turn[...], blk.reshape(256, 256)).astype(BF).reshape(16, 16, 256)
        if to_rows:
            dst[cols, at, :] = o
        else:
            dst[at, cols, :] = o

    def gate_two(src, dst, w, n):
        o = dot(w[...], planes_down(src[n], src[n + 1])).astype(BF)
        dst[n] = planes_up(o, 0)
        dst[n + 1] = planes_up(o, 1)

    def gate_one(src, dst, w, n):
        o = dot(src[pl.ds(n, 2)].reshape(256, 256), w[...]).astype(BF)
        dst[pl.ds(n, 2)] = o.reshape(2, 128, 256)

    s_here = (z + 6) % NZ
    part_here = s_here // 4

    def back(half):
        z_to = 4 * half + s_here % 4
        return pltpu.make_async_remote_copy(
            src_ref=sg.at[pl.ds(16 * half, 16)], dst_ref=sgr.at[part_here],
            send_sem=s_ss.at[half], recv_sem=s_rs.at[part_here],
            device_id=device(0, 0, z_to + NZ - z, 0), device_id_type=MESH)

    for half in range(2):
        def turned(i, carry, half=half):
            turn_block(b2, b2t, half, i, True)
            return carry

        def gates(i, carry, half=half):
            n = 16 * half + 2 * i
            gate_two(b2t, b1t, w2b, n)
            gate_one(b1t, sg, w1b, n)
            return carry

        lax.fori_loop(0, 8, turned, 0)
        lax.fori_loop(0, 8, gates, 0)
        back(half).start()

    def x_arrive(t, carry):
        x_copy(t).wait_recv()
        return carry

    own_x.wait()
    lax.fori_loop(1, 64, x_arrive, 0)

    for half in range(2):
        def x_turned(i, carry, half=half):
            turn_block(xq, xt, half, i, True)
            return carry

        lax.fori_loop(0, 8, x_turned, 0)

    def layers(i, carry):
        gate_one(xt, l1t, w1f, 2 * i)
        gate_two(l1t, l2t, w2f, 2 * i)
        return carry

    lax.fori_loop(0, 16, layers, 0)

    for half in range(2):
        def l_turned(i, carry, half=half):
            turn_block(l2t, b2, half, i, False)
            return carry

        lax.fori_loop(0, 8, l_turned, 0)

    def grad_two(n, acc):
        return acc + dot_nt(b2t[n], with_turned(l1t[n]))

    acc = lax.fori_loop(0, 32, grad_two, jnp.zeros((128, 256), F32))
    e[256:384, :] = acc[:, :128]
    e[384:512, :] = acc[:, 128:]

    v1acc[...] = jnp.zeros_like(v1acc)

    def grad_one(i, carry):
        rows = pl.ds(4 * i, 4)
        v1acc[...] += dot_tn(b1t[rows].reshape(512, 256), xt[rows].reshape(512, 256))
        return carry

    lax.fori_loop(0, 8, grad_one, 0)
    e[0:128, :] = v1acc[0:128, 0:128] + v1acc[128:256, 128:256]
    e[128:256, :] = v1acc[128:256, 0:128] - v1acc[0:128, 128:256]

    def grad_three(i, acc):
        for p in range(4):
            m = 4 * i + p
            acc = acc + dot_nt(call[m], with_turned(b2[m]))
        return acc

    acc3 = lax.fori_loop(0, 32, grad_three, jnp.zeros((128, 64), F32))
    acc3 = jnp.transpose(jnp.concatenate([acc3, jnp.zeros((128, 64), F32)], axis=1))
    e[512:768, :] = jnp.zeros((256, 128), F32)
    spot = pl.multiple_of(32 * x, 32)
    e[pl.ds(512 + spot, 32), :] = acc3[0:32, :]
    e[pl.ds(640 + spot, 32), :] = acc3[32:64, :]

    def one(dx):
        to = (x + dx) % NX
        return pltpu.make_async_remote_copy(
            src_ref=e.at[pl.ds(pl.multiple_of(192 * to, 192), 192), :], dst_ref=rx.at[x],
            send_sem=e1s.at[dx], recv_sem=e1r.at[dx], device_id=device(dx, 0, 0, 0), device_id_type=MESH)

    def yc(k):
        return ((y + k // 2) % NY) * 2 + (c + k % 2) % NC

    def two(k):
        to = yc(k)
        return pltpu.make_async_remote_copy(
            src_ref=ryc.at[8, pl.ds(pl.multiple_of(24 * to, 8), 24), :],
            dst_ref=ryc.at[y * 2 + c, pl.ds(0, 24), :],
            send_sem=e2s.at[k], recv_sem=e2r.at[k], device_id=device(0, k // 2, 0, k % 2), device_id_type=MESH)

    def three(dz):
        return pltpu.make_async_remote_copy(
            src_ref=rz.at[z], dst_ref=rz.at[z],
            send_sem=e3s.at[dz], recv_sem=e3r.at[dz], device_id=device(0, 0, dz, 0), device_id_type=MESH)

    def four(k):
        rows = fin.at[pl.ds(pl.multiple_of(192 * x + 24 * (y * 2 + c), 8), 24), :]
        return pltpu.make_async_remote_copy(
            src_ref=rows, dst_ref=rows,
            send_sem=e4s.at[k], recv_sem=e4r.at[k], device_id=device(0, k // 2, 0, k % 2), device_id_type=MESH)

    def five(dx):
        rows = fin.at[pl.ds(pl.multiple_of(192 * x, 192), 192), :]
        return pltpu.make_async_remote_copy(
            src_ref=rows, dst_ref=rows,
            send_sem=e5s.at[dx], recv_sem=e5r.at[dx], device_id=device(dx, 0, 0, 0), device_id_type=MESH)

    for dx in range(1, NX):
        one(dx).start()
    rx[x] = e[pl.ds(pl.multiple_of(192 * x, 192), 192), :]
    for dx in range(1, NX):
        one(dx).wait_recv()
    ryc[8] = (rx[0] + rx[1]) + (rx[2] + rx[3])
    for k in range(1, 8):
        two(k).start()
    ryc[y * 2 + c, 0:24, :] = ryc[8, pl.ds(pl.multiple_of(24 * (y * 2 + c), 8), 24), :]
    for k in range(1, 8):
        two(k).wait_recv()
    total = ryc[0, 0:24, :]
    for k in range(1, 8):
        total = total + ryc[k, 0:24, :]
    rz[z] = total
    for dz in range(1, NZ):
        three(dz).start()
    for dz in range(1, NZ):
        three(dz).wait_recv()
    total = rz[0]
    for k in range(1, NZ):
        total = total + rz[k]
    fin[pl.ds(pl.multiple_of(192 * x + 24 * (y * 2 + c), 8), 24), :] = total
    for k in range(1, 8):
        four(k).start()
    for k in range(1, 8):
        four(k).wait_recv()
    for dx in range(1, NX):
        five(dx).start()
    for dx in range(1, NX):
        five(dx).wait_recv()

    def exact(a, b, dims):
        return lax.dot_general(a, b, (dims, ((), ())), precision=HIGH, preferred_element_type=F32)

    factor = 1.0 / (128 * 64**0.5)
    for q in range(2):
        for s in range(2):
            part = fin[256 * s + 128 * q:256 * s + 128 * q + 128, :]
            moved = exact(pickers[s], part, ((0,), (0,)))
            eout[s, q] = exact(moved, pickers[s], ((1,), (0,))) * factor
        part = fin[512 + 128 * q:640 + 128 * q, :]
        moved = exact(pickers[2], part, ((0,), (1,)))
        eout[2, q] = exact(moved, pickers[2], ((1,), (0,))) * factor

    def c_gone(t, carry):
        c_copy(t).wait_send()
        x_copy(t).wait_send()
        return carry

    lax.fori_loop(1, 64, c_gone, 0)

    def g_gone(g, carry):
        for way in range(2):
            near(g, way).wait_send()
            far(g, way).wait_send()
        return carry

    lax.fori_loop(0, 8, g_gone, 0)
    for dx in range(1, NX):
        one(dx).wait_send()
        five(dx).wait_send()
    for k in range(1, 8):
        two(k).wait_send()
        three(k).wait_send()
        four(k).wait_send()

    def landed(part):
        return pltpu.make_async_remote_copy(
            src_ref=sg.at[pl.ds(0, 16)], dst_ref=sgr.at[part],
            send_sem=s_ss.at[0], recv_sem=s_rs.at[part],
            device_id=device(0, 0, 2, 0), device_id_type=MESH)

    landed(0).wait_recv()
    landed(1).wait_recv()

    def give(i, carry):
        n, hh = 2 * (i // 2), i % 2
        rows = pl.ds(pl.multiple_of(64 * hh, 64), 64)
        sides = []
        for nn in range(2):
            sides.append(jnp.concatenate(
                [sgr[r, n + nn, rows, cc * 128:cc * 128 + 128] for r in range(2) for cc in range(2)], axis=0))
        o = dot(outturn[...], jnp.concatenate(sides, axis=1)).astype(BF)
        at = pl.ds(pl.multiple_of(256 * hh, 256), 256)
        out[n, at, :] = o[:, :128]
        out[n + 1, at, :] = o[:, 128:]
        return carry

    lax.fori_loop(0, 16, give, 0)
    back(0).wait_send()
    back(1).wait_send()


def local(initial_state, cotangent, gate_bank, slice_index, mode_order):
    mats = [gate_matrix(gate_bank, slice_index, mode_order, number) for number in range(3)]
    first, second, third = mats[0][0], mats[1][0], mats[2][0]
    order = stored_order()
    second = second.reshape(2, 4, 4, 2, 4, 2, 4, 4, 2, 4).transpose(0, 1, 3, 2, 4, 5, 6, 8, 7, 9).reshape(256, 256)
    x = lax.axis_index("grp") // 2
    own = lax.dynamic_slice_in_dim(third, 32 * x, 32, 3)
    w3b = own.transpose(2, 3, 0, 1).reshape(64, 256)
    first = first.reshape(256, 256)
    pick_two = mats[1][1].reshape(4, 4, 2, 4, 128).transpose(0, 2, 1, 3, 4).reshape(128, 128)
    pickers = jnp.stack([mats[0][1], pick_two, mats[2][1]])
    del order
    vm = pl.BlockSpec(memory_space=pltpu.VMEM)
    big = lambda *shape: pltpu.VMEM(shape, BF)
    sem = lambda *shape: pltpu.SemaphoreType.DMA(shape)
    out, grads = pl.pallas_call(
        kernel,
        out_shape=(jax.ShapeDtypeStruct((16, 512, 128), BF), jax.ShapeDtypeStruct((3, 2, 128, 128), F32)),
        in_specs=[vm] * 10,
        out_specs=(vm, vm),
        scratch_shapes=[
            big(64, 4, 16, 256), big(64, 4, 16, 256), big(128, 128, 256), big(128, 32, 256),
            big(128, 32, 256), big(32, 128, 256), big(32, 128, 256), big(32, 128, 256),
            big(32, 128, 256), big(32, 128, 256), big(32, 128, 256), big(2, 16, 128, 256),
            pltpu.VMEM((256, 256), F32), pltpu.VMEM((768, 128), F32), pltpu.VMEM((4, 192, 128), F32),
            pltpu.VMEM((9, 192, 128), F32), pltpu.VMEM((8, 24, 128), F32), pltpu.VMEM((768, 128), F32),
            sem(64), sem(64), sem(64), sem(64), sem(2), sem(2, 8), sem(2, 8), sem(2, 8), sem(2, 8), sem(2), sem(2),
            sem(4), sem(4), sem(8), sem(8), sem(8), sem(8), sem(8), sem(8), sem(4), sem(4),
        ],
        compiler_params=pltpu.CompilerParams(collective_id=0, has_side_effects=True, vmem_limit_bytes=56 << 20),
        name="gradients",
    )(
        cotangent.reshape(16, 4, 128, 128), initial_state.reshape(16, 4, 128, 128),
        first.T, first, second, second.T, w3b,
        jnp.asarray(block_turn(), BF), jnp.asarray(output_turn(), BF), pickers,
    )
    return grads, out.reshape(16, 128, 2, 2, 128)


def solution(mesh):
    in_specs = (P("grp", "mem", None, None, None), P("grp", "mem", None, None, None), P(), P(), P())
    out_specs = (P(), P("grp", None, "mem", None, None))
    return jax.shard_map(local, mesh=mesh, in_specs=in_specs, out_specs=out_specs, check_vma=False)
```

time: 615 us -> 235 us (0.38)
  waiting for transfers between devices: 443 us -> 0 us
  Pallas kernels: 0 us -> 178 us
  blocking collectives: 60.3 us -> 0 us
  starting transfers between devices: 35.4 us -> 0 us
  between operations: 20.2 us -> 6.6 us
  matrix products: 11.9 us -> 1.11 us
    psum x1 -> x0, waiting for transfers between devices: 240 us -> none  [local(): totals = lax.psum((grad_one, grad_two, grad_three), ('grp', 'mem'))]
    all_to_all x5 -> x0, waiting for transfers between devices: 203 us -> none  [the longest x1 42.8 us: local(): lax.all_to_all(back_one, 'mem', split_axis=1, concat_axis=2, tiled=True)]
    pallas_call x0 -> x1, Pallas kernels: none -> 178 us  [local(): pl.pallas_call(kernel, out_shape=(jax.ShapeDtypeStruct((16, 512, 128), BF...]
    all_to_all x1 -> x0, blocking collectives: 60.3 us -> none  [local(): lax.all_to_all(cotangent, 'mem', split_axis=2, concat_axis=1, tiled=True)]
    all_to_all x5 -> x0, starting transfers between devices: 35.1 us -> none  [the longest x1 11 us: local(): lax.all_to_all(back_one, 'mem', split_axis=1, concat_axis=2, tiled=True)]
    convert_element_type x4 -> x0, local copies, waits for them, and re-layouts: 13.5 us -> none  [the longest x1 3.56 us: local(): contract('nirck,cidj->njrdk', back_middle, second).astype(jnp.bfloat16)]
    all_to_all x7 -> x0, local copies, waits for them, and re-layouts: 12.6 us -> none  [the longest x1 4.09 us: local(): lax.all_to_all(back_one, 'mem', split_axis=1, concat_axis=2, tiled=True)]
    another operation x3, local copies, waits for them, and re-layouts: 0.04 us -> 12 us  [the longest x2 11.9 us: gate_matrix(): upper = jnp.stack([moved[0], -moved[1]], axis=1)]
  transfers between devices with their start and end apart: 6 -> 0, of which waited for: 6 -> 0; matrix products, arithmetic and copies ran while one was open for 5% -> 0% of each run, Pallas kernels for 0% -> 0%
where the time goes in v1:
time: 235 us
  Pallas kernels  178 us (76%)
  local copies, waits for them, and re-layouts  43.1 us (18%)
  between operations  6.6 us (3%)
  other arithmetic  6 us (3%)
    pallas_call x1, Pallas kernels, local(): pl.pallas_call(kernel, out_shape=(jax.ShapeDtypeStruct((16, 512, 128), BF...  178 us
    another operation x2, local copies, waits for them, and re-layouts, gate_matrix(): upper = jnp.stack([moved[0], -moved[1]], axis=1)  11.9 us
    squeeze x4, local copies, waits for them, and re-layouts, gate_matrix(): upper = jnp.stack([moved[0], -moved[1]], axis=1)  10.2 us
    reshape x2, local copies, waits for them, and re-layouts, local(): second.reshape(2, 4, 4, 2, 4, 2, 4, 4, 2, 4)  9.66 us
    unnamed x8, local copies, waits for them, and re-layouts  6.85 us

profile of v1, /device:TPU:1, one launch (start us, length us, event | category | flops | bytes accessed | tf_op | source)
XLA Modules:
  0.0 234.8 jit_solution(857914928930886439)
XLA Ops:
  0.6 1.4 fusion.58
  4.0 0.8 slice_bitcast_fusion.4
  4.8 0.1 shift-left_reduce_fusion
  4.9 1.2 fusion.56
  6.0 0.4 fusion.9
  6.5 0.6 copy.34
  9.1 0.1 shift-left_reduce_fusion.2
  9.2 0.4 fusion.12
  9.6 0.1 copy.18
  9.8 0.0 copy-start.1
  9.8 0.8 copy.25.w1f
  12.4 0.3 fusion.15
  12.8 2.2 squeeze.36
  15.0 7.9 %copy.19 = bf16[1,4,4,2,4,1,4,4,2,4]{4,2,3,1,0,9,7,8,6,5:T(4,128)(2,1)S(1)} copy(bf16[1,4,4,2,4,1,4,4,2,4]{9,8,7,6,4,3,2,1,5,0:T(2,128)(2,1)S(1)} %squeeze.36) | data formatting | bytes 65536 | tf_op jit(solution)/shard_map/squeeze | solution.py:59
  22.9 0.7 neg.32
  23.6 3.2 %stack.58 = bf16[1,4,4,2,4,1,4,4,2,4]{9,8,7,6,4,3,2,1,5,0:T(2,128)(2,1)} reshape(bf16[1,128,128]{2,1,0:T(8,128)(2,1)S(1)} %get-tuple-element.14) | data formatting | bytes 65536 | tf_op jit(solution)/shard_map/stack | solution.py:59
  26.9 8.7 %copy.20 = bf16[1,4,4,2,4,1,4,4,2,4]{4,2,3,1,0,9,7,8,6,5:T(4,128)(2,1)S(1)} copy(bf16[1,4,4,2,4,1,4,4,2,4]{9,8,7,6,4,3,2,1,5,0:T(2,128)(2,1)} %stack.58) | data formatting | bytes 65536 | tf_op jit(solution)/shard_map/stack | solution.py:59
  35.6 0.0 copy-done.1
  35.6 4.1 %maximum_bitcast_fusion = bf16[2,4,2,4,4,2,4,2,4,4]{4,3,2,1,0,9,8,7,6,5:T(4,128)(2,1)} fusion(bf16[1,4,4,2,4,1,4,4,2,4]{4,2,3,1,0,9,7,8,6,5:T(4,128)(2,1)S(1)} %copy.20, bf16[1,4,4,2,4,1,4,4,2,4]{4,2,3,1,0,9,7,8,6,5:T(4,128)(2,1)S(1)} %copy.19, bf16[1,4,4,2,4,1,4,4,2,4]{4,2,3,1,0,9,7,8,6,5:T(4,128)(2,1)S(1)} %neg.32), kind=kLoop, calls=%fused_computation | loop fusion | flops 196608 | bytes 229376 | tf_op jit(solution)/shard_map/transpose | solution.py:488
  39.6 8.9 %reshape.165 = bf16[256,256]{0,1:T(8,128)(2,1)S(1)} reshape(bf16[2,4,2,4,4,2,4,2,4,4]{4,3,2,1,0,9,8,7,6,5:T(4,128)(2,1)} %maximum_bitcast_fusion) | data formatting | bytes 262144 | tf_op jit(solution)/shard_map/reshape | solution.py:488
  48.5 0.0 copy-start
  48.6 0.8 copy.26.w2f
  49.3 0.1 eq.96
  49.5 0.1 eq.98
  49.6 0.1 iota_compare_fusion.1
  49.7 0.1 iota_compare_fusion
  49.8 0.1 iota_compare_fusion.2
  49.8 0.7 add_convert_fusion.pickers
  50.5 0.0 copy-done
  50.5 178.0 %gradients.1 = (bf16[16,512,128]{2,1,0:T(8,128)(2,1)}, f32[3,2,128,128]{3,2,1,0:T(8,128)}) custom-call(bf16[16,4,128,128]{3,2,1,0:T(8,128)(2,1)} %bitcast.78, bf16[16,4,128,128]{3,2,1,0:T(8,128)(2,1)} %bitcast.79, bf16[256,256]{1,0:T(8,128)(2,1)} %copy.25.w1f, bf16[256,256]{1,0:T(8,128)(2,1)} %bitcast.83, bf16[256,256]{1,0:T(8,128)(2,1)} %copy.26.w2f, ...), custom_call_target="tpu_custom_call" | custom-call | tf_op jit(solution)/shard_map/gradients/pallas_call | solution.py:499
  228.6 1.8 copy.37
  230.4 4.4 %copy.38 = bf16[16,128,2,2,128]{4,3,2,1,0:T(2,128)(2,1)} copy(bf16[16,128,2,2,128]{4,3,2,1,0:T(2,128)(2,1)} %bitcast.80) | data formatting | bytes 4194304
  (12 shorter events, 0.2 us)
Async XLA Ops:
  9.8 25.8 %copy-start.1 = (bf16[32,8,2,128]{3,1,2,0:T(8,128)(2,1)}, bf16[32,8,2,128]{3,1,2,0:T(8,128)(2,1)S(1)}, u32[]{:S(2)}) copy-start(bf16[32,8,2,128]{3,1,2,0:T(8,128)(2,1)S(1)} %copy.33) | copy-start | bytes 393220
  48.5 2.0 copy-start

commit v2 on v1

v2 whole, which is shorter than its diff:
```python
import jax
import jax.numpy as jnp
from jax import lax
from jax.experimental import pallas as pl
from jax.experimental.pallas import tpu as pltpu
from jax.sharding import PartitionSpec as P

MESH = pl.DeviceIdType.MESH
BF = jnp.bfloat16
F32 = jnp.float32
HIGH = lax.Precision.HIGHEST
NX, NY, NZ, NC = 4, 4, 8, 2
Z_ORDER = (4, 3, 5, 2, 6, 1, 7, 0)
X_LAG = 0
FINISH_MIB = 60
PIECES = 4
EARLY = 2


def grid(shape):
    return lax.broadcasted_iota(jnp.int32, shape, 0), lax.broadcasted_iota(jnp.int32, shape, 1)


def block_turn():
    row, col = grid((256, 256))
    return ((row & 15) * 16 + (row >> 4) == col).astype(F32).astype(BF)


def output_turn():
    row, col = grid((256, 256))
    m = row >> 2
    stored = (m & 35) + ((m >> 2) & 1) * 16 + ((m >> 3) & 3) * 4
    return ((row & 3) * 64 + stored == col).astype(F32).astype(BF)


def index_table(order, number, stored):
    row, col = grid((128, 128))
    if stored:
        row = (row & 99) + ((row >> 4) & 1) * 4 + ((row >> 2) & 3) * 8
    mapped = jnp.zeros((128, 128), jnp.int32)
    for b in range(7):
        mapped = mapped + (((row >> b) & 1) << order[number, b])
    return (mapped == col).astype(F32)


def dot(a, b):
    return jnp.dot(a, b, preferred_element_type=F32)


def dot_nt(a, b):
    return lax.dot_general(a, b, (((1,), (1,)), ((), ())), preferred_element_type=F32)


def dot_tn(a, b):
    return lax.dot_general(a, b, (((0,), (0,)), ((), ())), preferred_element_type=F32)


def planes_down(a, b):
    top = jnp.concatenate([a[:, :128], b[:, :128]], axis=1)
    low = jnp.concatenate([a[:, 128:], b[:, 128:]], axis=1)
    return jnp.concatenate([top, low], axis=0)


def planes_up(o, which):
    half = o.shape[0] // 2
    lanes = slice(128 * which, 128 * which + 128)
    return jnp.concatenate([o[:half, lanes], o[half:, lanes]], axis=1)


def with_turned(l):
    return jnp.concatenate([l, jnp.concatenate([-l[:, 128:], l[:, :128]], axis=1)], axis=0)


def batches(count, size, load, compute, store):
    def body(i, carry):
        made = [compute(v) for v in [load(i * size + u) for u in range(size)]]
        for u in range(size):
            store(i * size + u, made[u])
        return carry

    lax.fori_loop(0, count // size, body, 0)


def kernel(
    c_in, x_in, bank_in, slices, order,
    sgr, eout,
    craw, xraw, bank, pickers,
    w1f, w1b, w2f, w2b, w3b, w3all, turn,
    csend, xsend, call, xq, b2, b2t, b1t, sg, xt, l1t, l2t, e, rx, ryc, rz, fin,
    in_s, c_ss, c_rs, x_ss, x_rs, loc, g_ss, g_rs, f_ss, f_rs, s_ss, s_rs,
    e1s, e1r, e2s, e2r, e3s, e3r, e4s, e4r, e5s, e5r,
):
    grp, mem = lax.axis_index("grp"), lax.axis_index("mem")
    x, zh = grp // 2, grp % 2
    y, zl, c = mem // 8, (mem // 2) % 4, mem % 2
    z = zh * 4 + zl

    def device(dx, dy, dz, dc):
        x2, y2, z2, c2 = (x + dx) % NX, (y + dy) % NY, (z + dz) % NZ, (c + dc) % NC
        return (x2 * 2 + z2 // 4, (y2 * 4 + z2 % 4) * 2 + c2)

    def yzc(t):
        return t // 16, t % 8, (t // 8) % 2

    loads = [pltpu.make_async_copy(a, b, in_s.at[i]) for i, (a, b) in enumerate(((c_in, craw), (x_in, xraw), (bank_in, bank)))]
    for load in loads:
        load.start()
    bar = pltpu.get_barrier_semaphore()

    def greet(t, carry):
        dy, dz, dc = yzc(t)
        pl.semaphore_signal(bar, inc=1, device_id=device(0, dy, dz, dc), device_id_type=MESH)
        return carry

    lax.fori_loop(1, 64, greet, 0)
    for dx in range(1, NX):
        pl.semaphore_signal(bar, inc=1, device_id=device(dx, 0, 0, 0), device_id_type=MESH)

    def extract(raw, send):
        def load(i):
            mp, rb = i // 8, i % 8
            rows = pl.ds(pl.multiple_of(16 * rb, 16), 16)
            return jnp.concatenate([raw[:, 2 * mp + mm, rows, :].reshape(256, 128) for mm in range(2)], axis=1)

        def store(i, o):
            mp, rb = i // 8, i % 8
            for mm in range(2):
                for r in range(8):
                    for cc in range(2):
                        q = (r * 2 + cc) * 16
                        send[8 * rb + r, 2 * mp + mm, :, cc * 128:cc * 128 + 128] = o[q:q + 16, mm * 128:mm * 128 + 128]

        batches(16, 8, load, lambda v: dot(turn[...], v).astype(BF), store)

    turn[...] = block_turn()
    loads[0].wait()
    extract(craw, csend)
    pl.semaphore_wait(bar, 66)

    def make_gates():
        for s in range(3):
            pickers[s] = index_table(order, s, s == 1)
            small = pickers[s].astype(BF)
            planes, turned = [], []
            for q in range(2):
                chosen = bank[s, slices[s], q]
                planes.append(dot_nt(dot(small, chosen).astype(BF), small).astype(BF))
                turned.append(dot_nt(dot_nt(small, chosen).astype(BF), small).astype(BF))
            whole, flipped = ((w1b, w1f), (w2f, w2b), (None, w3all))[s]
            if whole is not None:
                whole[0:128, 0:128] = planes[0]
                whole[0:128, 128:256] = -planes[1]
                whole[128:256, 0:128] = planes[1]
                whole[128:256, 128:256] = planes[0]
            flipped[0:128, 0:128] = turned[0]
            flipped[0:128, 128:256] = turned[1]
            flipped[128:256, 0:128] = -turned[1]
            flipped[128:256, 128:256] = turned[0]
        at = pl.multiple_of(32 * x, 32)
        w3b[0:32, :] = w3all[pl.ds(at, 32), :]
        w3b[32:64, :] = w3all[pl.ds(128 + at, 32), :]

    m_own = pl.multiple_of(y * 32 + c * 16 + zl * 4, 4)

    def part_of(dy, dz, dc):
        s = (z + dz + 6) % NZ
        return 2 * ((((y + dy) % NY) * 4 + s % 4) * 2 + (c + dc) % NC) + s // 4

    def c_copy(t):
        dy, dz, dc = yzc(t)
        return pltpu.make_async_remote_copy(
            src_ref=csend.at[part_of(dy, dz, dc)],
            dst_ref=call.at[grp, pl.ds(m_own, 4)],
            send_sem=c_ss.at[t], recv_sem=c_rs.at[t],
            device_id=device(0, dy, dz, dc), device_id_type=MESH)

    def x_copy(t):
        dy, dz, dc = yzc(t)
        return pltpu.make_async_remote_copy(
            src_ref=xsend.at[part_of(dy, dz, dc)],
            dst_ref=xq.at[zh, pl.ds(m_own, 4)],
            send_sem=x_ss.at[t], recv_sem=x_rs.at[t],
            device_id=device(0, dy, dz, dc), device_id_type=MESH)

    own_c = pltpu.make_async_copy(csend.at[part_of(0, 0, 0)], call.at[grp, pl.ds(m_own, 4)], loc.at[0])
    own_x = pltpu.make_async_copy(xsend.at[part_of(0, 0, 0)], xq.at[zh, pl.ds(m_own, 4)], loc.at[1])

    def start_group(copy, g):
        for dz in Z_ORDER:
            if dz == 0:
                @pl.when(g > 0)
                def _():
                    copy(g * 8).start()
            else:
                copy(g * 8 + dz).start()

    def c_start(g, carry):
        start_group(c_copy, g)
        return carry

    def x_start(g, carry):
        start_group(x_copy, g)
        return carry

    own_c.start()
    lax.fori_loop(0, 8, c_start, 0)
    loads[1].wait()
    extract(xraw, xsend)
    own_x.start()
    if X_LAG < 0:
        lax.fori_loop(0, 8, x_start, 0)
    loads[2].wait()
    make_gates()

    def m_of(g):
        dy, dc = g // 2, g % 2
        return pl.multiple_of(((y + NY - dy) % NY) * 32 + ((c + NC - dc) % NC) * 16, 16)

    def near(g, way):
        part = call.at[pl.ds(2 * x, 2), pl.ds(m_of(g), 16)]
        return pltpu.make_async_remote_copy(
            src_ref=part, dst_ref=part, send_sem=g_ss.at[way, g], recv_sem=g_rs.at[way, g],
            device_id=device(1 if way == 0 else NX - 1, 0, 0, 0), device_id_type=MESH)

    def far(g, way):
        owner = (x + NX - 1) % NX if way == 0 else (x + 1) % NX
        part = call.at[pl.ds(2 * owner, 2), pl.ds(m_of(g) + 8 * way, 8)]
        return pltpu.make_async_remote_copy(
            src_ref=part, dst_ref=part, send_sem=f_ss.at[way, g], recv_sem=f_rs.at[way, g],
            device_id=device(1 if way == 0 else NX - 1, 0, 0, 0), device_id_type=MESH)

    def relay(g):
        for way in range(2):
            near(g, way).wait_recv()
            far(g, way).start()

    def arrive(g, carry):
        for dz in Z_ORDER:
            if dz == 0:
                @pl.when(g > 0)
                def _():
                    c_copy(g * 8).wait_recv()
            else:
                c_copy(g * 8 + dz).wait_recv()

        @pl.when(g == 0)
        def _():
            own_c.wait()

        near(g, 0).start()
        near(g, 1).start()

        if X_LAG >= 0:
            @pl.when(g >= X_LAG)
            def _():
                start_group(x_copy, g - X_LAG)

        @pl.when(g >= 1)
        def _():
            relay(g - 1)

        return carry

    lax.fori_loop(0, 8, arrive, 0)
    if X_LAG > 0:
        lax.fori_loop(8 - X_LAG, 8, x_start, 0)
    relay(7)

    def all_n(m):
        return call[:, m].reshape(128, 256)

    def third(g, carry):
        far(g, 0).wait_recv()
        far(g, 1).wait_recv()

        base = m_of(g)
        made = [planes_down(all_n(base + 2 * p), all_n(base + 2 * p + 1)) for p in range(8)]
        made = [dot(w3b[...], v).astype(BF) for v in made]
        for p in range(8):
            b2[base + 2 * p] = planes_up(made[p], 0)
            b2[base + 2 * p + 1] = planes_up(made[p], 1)
        return carry

    lax.fori_loop(0, 8, third, 0)

    def turn_all(src, dst, to_rows):
        def places(i):
            return pl.ds(pl.multiple_of(16 * (i % 8), 16), 16), pl.ds(pl.multiple_of(16 * (i // 8), 16), 16)

        def load(i):
            m, n = places(i)
            if len(src.shape) == 4:
                return src[i // 8, m].reshape(256, 256)
            return (src[m, n, :] if to_rows else src[n, m, :]).reshape(256, 256)

        def store(i, o):
            m, n = places(i)
            if to_rows:
                dst[n, m, :] = o.reshape(16, 16, 256)
            else:
                dst[m, n, :] = o.reshape(16, 16, 256)

        batches(16, 8, load, lambda v: dot(turn[...], v).astype(BF), store)

    def gate_two(src, dst, w, base, pairs):
        def store(i, o):
            dst[base + 2 * i] = planes_up(o, 0)
            dst[base + 2 * i + 1] = planes_up(o, 1)

        batches(pairs, 4, lambda i: planes_down(src[base + 2 * i], src[base + 2 * i + 1]),
                lambda v: dot(w[...], v).astype(BF), store)

    def gate_one(src, dst, w, base, pairs):
        def store(i, o):
            dst[pl.ds(base + 2 * i, 2)] = o.reshape(2, 128, 256)

        batches(pairs, 4, lambda i: src[pl.ds(base + 2 * i, 2)].reshape(256, 256),
                lambda v: dot(v, w[...]).astype(BF), store)

    s_here = (z + 6) % NZ
    part_here = s_here // 4

    per = 16 // PIECES

    def back(half, k):
        z_to = 4 * half + s_here % 4
        return pltpu.make_async_remote_copy(
            src_ref=sg.at[pl.ds(16 * half + per * k, per)], dst_ref=sgr.at[part_here, pl.ds(per * k, per)],
            send_sem=s_ss.at[half, k], recv_sem=s_rs.at[part_here, k],
            device_id=device(0, 0, z_to + NZ - z, 0), device_id_type=MESH)

    turn_all(b2, b2t, True)
    for k in range(2):
        for half in range(2):
            n = 16 * half + 8 * k
            gate_two(b2t, b1t, w2b, n, 4)
            gate_one(b1t, sg, w1b, n, 4)
        for j in range(PIECES // 2 * k, PIECES // 2 * (k + 1)):
            if j < EARLY:
                back(0, j).start()
                back(1, j).start()

    def x_arrive(t, carry):
        x_copy(t).wait_recv()
        return carry

    own_x.wait()
    lax.fori_loop(1, 64, x_arrive, 0)

    turn_all(xq, xt, True)
    gate_one(xt, l1t, w1f, 0, 16)
    gate_two(l1t, l2t, w2f, 0, 16)
    turn_all(l2t, b2, False)

    def grad_two(i, acc):
        for u in range(8):
            acc = acc + dot_nt(b2t[8 * i + u], with_turned(l1t[8 * i + u]))
        return acc

    acc = lax.fori_loop(0, 4, grad_two, jnp.zeros((128, 256), F32))
    e[256:384, :] = acc[:, :128]
    e[384:512, :] = acc[:, 128:]

    def grad_one(i, acc):
        rows = pl.ds(8 * i, 8)
        return acc + dot_tn(b1t[rows].reshape(1024, 256), xt[rows].reshape(1024, 256))

    acc = lax.fori_loop(0, 4, grad_one, jnp.zeros((256, 256), F32))
    e[0:128, :] = acc[0:128, 0:128] + acc[128:256, 128:256]
    e[128:256, :] = acc[128:256, 0:128] - acc[0:128, 128:256]

    def grad_three(i, acc):
        for p in range(16):
            acc = acc + dot_nt(all_n(16 * i + p), with_turned(b2[16 * i + p]))
        return acc

    acc3 = lax.fori_loop(0, 8, grad_three, jnp.zeros((128, 64), F32))
    acc3 = jnp.transpose(jnp.concatenate([acc3, jnp.zeros((128, 64), F32)], axis=1))
    e[512:768, :] = jnp.zeros((256, 128), F32)
    spot = pl.multiple_of(32 * x, 32)
    e[pl.ds(512 + spot, 32), :] = acc3[0:32, :]
    e[pl.ds(640 + spot, 32), :] = acc3[32:64, :]

    def one(dx):
        to = (x + dx) % NX
        return pltpu.make_async_remote_copy(
            src_ref=e.at[pl.ds(pl.multiple_of(192 * to, 192), 192), :], dst_ref=rx.at[x],
            send_sem=e1s.at[dx], recv_sem=e1r.at[dx], device_id=device(dx, 0, 0, 0), device_id_type=MESH)

    def yc(k):
        return ((y + k // 2) % NY) * 2 + (c + k % 2) % NC

    def two(k):
        to = yc(k)
        return pltpu.make_async_remote_copy(
            src_ref=ryc.at[8, pl.ds(pl.multiple_of(24 * to, 8), 24), :],
            dst_ref=ryc.at[y * 2 + c, pl.ds(0, 24), :],
            send_sem=e2s.at[k], recv_sem=e2r.at[k], device_id=device(0, k // 2, 0, k % 2), device_id_type=MESH)

    def three(dz):
        return pltpu.make_async_remote_copy(
            src_ref=rz.at[z], dst_ref=rz.at[z],
            send_sem=e3s.at[dz], recv_sem=e3r.at[dz], device_id=device(0, 0, dz, 0), device_id_type=MESH)

    def four(k):
        rows = fin.at[pl.ds(pl.multiple_of(192 * x + 24 * (y * 2 + c), 8), 24), :]
        return pltpu.make_async_remote_copy(
            src_ref=rows, dst_ref=rows,
            send_sem=e4s.at[k], recv_sem=e4r.at[k], device_id=device(0, k // 2, 0, k % 2), device_id_type=MESH)

    def five(dx):
        rows = fin.at[pl.ds(pl.multiple_of(192 * x, 192), 192), :]
        return pltpu.make_async_remote_copy(
            src_ref=rows, dst_ref=rows,
            send_sem=e5s.at[dx], recv_sem=e5r.at[dx], device_id=device(dx, 0, 0, 0), device_id_type=MESH)

    for dx in range(1, NX):
        one(dx).start()
    rx[x] = e[pl.ds(pl.multiple_of(192 * x, 192), 192), :]
    for dx in range(1, NX):
        one(dx).wait_recv()
    ryc[8] = (rx[0] + rx[1]) + (rx[2] + rx[3])
    for k in range(1, 8):
        two(k).start()
    ryc[y * 2 + c, 0:24, :] = ryc[8, pl.ds(pl.multiple_of(24 * (y * 2 + c), 8), 24), :]
    for k in range(1, 8):
        two(k).wait_recv()
    total = ryc[0, 0:24, :]
    for k in range(1, 8):
        total = total + ryc[k, 0:24, :]
    rz[z] = total
    for dz in range(1, NZ):
        three(dz).start()
    for j in range(EARLY, PIECES):
        back(0, j).start()
        back(1, j).start()
    for dz in range(1, NZ):
        three(dz).wait_recv()
    total = rz[0]
    for k in range(1, NZ):
        total = total + rz[k]
    fin[pl.ds(pl.multiple_of(192 * x + 24 * (y * 2 + c), 8), 24), :] = total
    for k in range(1, 8):
        four(k).start()
    for k in range(1, 8):
        four(k).wait_recv()
    for dx in range(1, NX):
        five(dx).start()
    for dx in range(1, NX):
        five(dx).wait_recv()

    def exact(a, b, dims):
        return lax.dot_general(a, b, (dims, ((), ())), precision=HIGH, preferred_element_type=F32)

    factor = 1.0 / (128 * 64**0.5)
    sides = [(s, q) for s in range(3) for q in range(2)]
    moved = [exact(pickers[s], fin[256 * s + 128 * q:256 * s + 128 * q + 128, :], ((0,), (1,) if s == 2 else (0,))) for s, q in sides]
    for (s, q), part in zip(sides, moved):
        eout[s, q] = exact(part, pickers[s], ((1,), (0,))) * factor

    def c_gone(t, carry):
        c_copy(t).wait_send()
        x_copy(t).wait_send()
        return carry

    lax.fori_loop(1, 64, c_gone, 0)

    def g_gone(g, carry):
        for way in range(2):
            near(g, way).wait_send()
            far(g, way).wait_send()
        return carry

    lax.fori_loop(0, 8, g_gone, 0)
    for dx in range(1, NX):
        one(dx).wait_send()
        five(dx).wait_send()
    for k in range(1, 8):
        two(k).wait_send()
        three(k).wait_send()
        four(k).wait_send()

    def landed(part, k):
        return pltpu.make_async_remote_copy(
            src_ref=sg.at[pl.ds(0, per)], dst_ref=sgr.at[part, pl.ds(per * k, per)],
            send_sem=s_ss.at[0, k], recv_sem=s_rs.at[part, k],
            device_id=device(0, 0, 2, 0), device_id_type=MESH)

    for k in range(PIECES):
        for half in range(2):
            landed(half, k).wait_recv()
            back(half, k).wait_send()


def finish(sgr, sums, out, eout, outturn):
    @pl.when(pl.program_id(0) == 0)
    def _():
        outturn[...] = output_turn()
        eout[...] = sums[...]

    made = []
    for i in range(4):
        n, rows = 2 * (i // 2), slice(64 * (i % 2), 64 * (i % 2) + 64)
        sides = [jnp.concatenate([sgr[r, n + nn, rows, cc * 128:cc * 128 + 128] for r in range(2) for cc in range(2)], axis=0)
                 for nn in range(2)]
        made.append(dot(outturn[...], jnp.concatenate(sides, axis=1)).astype(BF))
    for i in range(4):
        n, at = 2 * (i // 2), slice(256 * (i % 2), 256 * (i % 2) + 256)
        out[n, at, :] = made[i][:, :128]
        out[n + 1, at, :] = made[i][:, 128:]


def local(initial_state, cotangent, gate_bank, slice_index, mode_order):
    hbm = pl.BlockSpec(memory_space=pl.ANY)
    vm = pl.BlockSpec(memory_space=pltpu.VMEM)
    sm = pl.BlockSpec(memory_space=pltpu.SMEM)
    big = lambda *shape: pltpu.VMEM(shape, BF)
    wide = lambda *shape: pltpu.VMEM(shape, F32)
    sem = lambda *shape: pltpu.SemaphoreType.DMA(shape)
    backs, sums = pl.pallas_call(
        kernel,
        out_shape=(jax.ShapeDtypeStruct((2, 16, 128, 256), BF), jax.ShapeDtypeStruct((3, 2, 128, 128), F32)),
        in_specs=[hbm, hbm, hbm, sm, sm],
        out_specs=(hbm, vm),
        scratch_shapes=[
            big(16, 4, 128, 128), big(16, 4, 128, 128), big(3, 4, 2, 128, 128), wide(3, 128, 128),
            big(256, 256), big(256, 256), big(256, 256), big(256, 256), big(64, 256), big(256, 256), big(256, 256),
            big(64, 4, 16, 256), big(64, 4, 16, 256), big(8, 128, 16, 256), big(2, 128, 16, 256),
            big(128, 32, 256), big(32, 128, 256), big(32, 128, 256), big(32, 128, 256),
            big(32, 128, 256), big(32, 128, 256), big(32, 128, 256),
            wide(768, 128), wide(4, 192, 128), wide(9, 192, 128), wide(8, 24, 128), wide(768, 128),
            sem(3), sem(64), sem(64), sem(64), sem(64), sem(2), sem(2, 8), sem(2, 8), sem(2, 8), sem(2, 8), sem(2, PIECES), sem(2, PIECES),
            sem(4), sem(4), sem(8), sem(8), sem(8), sem(8), sem(8), sem(8), sem(4), sem(4),
        ],
        compiler_params=pltpu.CompilerParams(collective_id=0, has_side_effects=True, vmem_limit_bytes=54 << 20),
        name="gradients",
    )(
        cotangent.reshape(16, 4, 128, 128), initial_state.reshape(16, 4, 128, 128),
        gate_bank, slice_index, mode_order,
    )
    out, grads = pl.pallas_call(
        finish,
        grid=(4,),
        out_shape=(jax.ShapeDtypeStruct((16, 512, 128), BF), jax.ShapeDtypeStruct((3, 2, 128, 128), F32)),
        in_specs=[
            pl.BlockSpec((2, 4, 128, 256), lambda i: (0, i, 0, 0)),
            pl.BlockSpec((3, 2, 128, 128), lambda i: (0, 0, 0, 0)),
        ],
        out_specs=(pl.BlockSpec((4, 512, 128), lambda i: (i, 0, 0)), pl.BlockSpec((3, 2, 128, 128), lambda i: (0, 0, 0, 0))),
        scratch_shapes=[big(256, 256)],
        compiler_params=pltpu.CompilerParams(vmem_limit_bytes=FINISH_MIB << 20),
        name="outputs",
    )(backs, sums)
    return grads, out.reshape(16, 128, 2, 2, 128)


def solution(mesh):
    in_specs = (P("grp", "mem", None, None, None), P("grp", "mem", None, None, None), P(), P(), P())
    out_specs = (P(), P("grp", None, "mem", None, None))
    return jax.shard_map(local, mesh=mesh, in_specs=in_specs, out_specs=out_specs, check_vma=False)
```

time: 235 us -> 167 us (0.71)
  local copies, waits for them, and re-layouts: 43.1 us -> 0 us
  Pallas kernels: 178 us -> 166 us
  other arithmetic: 6 us -> 0 us
  between operations: 6.6 us -> 0.64 us
    pallas_call x1 -> x2, Pallas kernels: 178 us -> 166 us  [the longest x1 161 us: local(): pl.pallas_call(kernel, out_shape=(jax.ShapeDtypeStruct((2, 16, 128, 256),...]
    another operation x3 -> x0, local copies, waits for them, and re-layouts: 12 us -> none  [the longest x2 11.9 us: gate_matrix(): upper = jnp.stack([moved[0], -moved[1]], axis=1)]
    squeeze x4 -> x0, local copies, waits for them, and re-layouts: 10.2 us -> none  [gate_matrix(): upper = jnp.stack([moved[0], -moved[1]], axis=1)]
    reshape x2 -> x0, local copies, waits for them, and re-layouts: 9.66 us -> none  [local(): second.reshape(2, 4, 4, 2, 4, 2, 4, 4, 2, 4)]
    unnamed x8 -> x0, local copies, waits for them, and re-layouts: 6.85 us -> none
    transpose x2 -> x0, other arithmetic: 4.09 us -> none  [the longest x1 4.08 us: local(): second.reshape(2, 4, 4, 2, 4, 2, 4, 4, 2, 4)]
    slice x3 -> x0, local copies, waits for them, and re-layouts: 2.55 us -> none  [the longest x1 1.38 us: gate_matrix(): slice_index[number]]
where the time goes in v2:
time: 167 us; the launch traced here: 166 us
  Pallas kernels  166 us (99%)
    pallas_call x1, Pallas kernels, local(): pl.pallas_call(kernel, out_shape=(jax.ShapeDtypeStruct((2, 16, 128, 256),...  161 us
    pallas_call x1, Pallas kernels, local(): pl.pallas_call(finish, grid=(4,), out_shape=(jax.ShapeDtypeStruct((16, 51...  4.54 us

profile of v2, /device:TPU:1, one launch (start us, length us, event | category | flops | bytes accessed | tf_op | source)
XLA Modules:
  0.0 166.4 jit_solution(2855238918602611398)
XLA Ops:
  0.6 161.2 %gradients.1 = (bf16[2,16,128,256]{3,2,1,0:T(8,128)(2,1)}, f32[3,2,128,128]{3,2,1,0:T(8,128)}) custom-call(bf16[16,4,128,128]{3,2,1,0:T(8,128)(2,1)} %bitcast.3, bf16[16,4,128,128]{3,2,1,0:T(8,128)(2,1)} %bitcast.4, bf16[3,4,2,128,128]{4,3,2,1,0:T(8,128)(2,1)} %bank_in.1, s32[3]{0:T(128)} %slices.1, s32[3,7]{1,0:T(4,128)} %order.1), custom_call_target="tpu_custom_call" | custom-call | tf_op jit(solution)/shard_map/gradients/pallas_call | solution.py:520
  161.9 4.5 %outputs.1 = (bf16[16,512,128]{2,1,0:T(8,128)(2,1)}, f32[3,2,128,128]{3,2,1,0:T(8,128)}) custom-call(bf16[2,16,128,256]{3,2,1,0:T(8,128)(2,1)} %get-tuple-element.6.sgr, f32[3,2,128,128]{3,2,1,0:T(8,128)} %get-tuple-element.7.sums), custom_call_target="tpu_custom_call" | custom-call | tf_op jit(solution)/shard_map/outputs/pallas_call | solution.py:541

commit v3 on v2

--- a/solution.py
+++ b/solution.py
@@ -11,10 +11,9 @@
 HIGH = lax.Precision.HIGHEST
 NX, NY, NZ, NC = 4, 4, 8, 2
 Z_ORDER = (4, 3, 5, 2, 6, 1, 7, 0)
-X_LAG = 0
-FINISH_MIB = 60
-PIECES = 4
-EARLY = 2
+PIECES = 8
+EARLY = 5
+STEPS = 2
 
 
 def grid(shape):
@@ -116,25 +115,24 @@
     for dx in range(1, NX):
         pl.semaphore_signal(bar, inc=1, device_id=device(dx, 0, 0, 0), device_id_type=MESH)
 
-    def extract(raw, send):
-        def load(i):
-            mp, rb = i // 8, i % 8
-            rows = pl.ds(pl.multiple_of(16 * rb, 16), 16)
-            return jnp.concatenate([raw[:, 2 * mp + mm, rows, :].reshape(256, 128) for mm in range(2)], axis=1)
-
-        def store(i, o):
-            mp, rb = i // 8, i % 8
+    def extract(raw, send, dy):
+        first = 2 * ((y + dy) % NY)
+        loaded = []
+        for i in range(4):
+            mp, rows = i // 2, pl.ds(pl.multiple_of(16 * (first + i % 2), 16), 16)
+            loaded.append(jnp.concatenate([raw[:, 2 * mp + mm, rows, :].reshape(256, 128) for mm in range(2)], axis=1))
+        made = [dot(turn[...], v).astype(BF) for v in loaded]
+        for i in range(4):
+            mp, r0 = i // 2, 8 * (first + i % 2)
             for mm in range(2):
                 for r in range(8):
                     for cc in range(2):
                         q = (r * 2 + cc) * 16
-                        send[8 * rb + r, 2 * mp + mm, :, cc * 128:cc * 128 + 128] = o[q:q + 16, mm * 128:mm * 128 + 128]
-
-        batches(16, 8, load, lambda v: dot(turn[...], v).astype(BF), store)
+                        send[r0 + r, 2 * mp + mm, :, cc * 128:cc * 128 + 128] = made[i][q:q + 16, mm * 128:mm * 128 + 128]
 
     turn[...] = block_turn()
     loads[0].wait()
-    extract(craw, csend)
+    extract(craw, csend, 0)
     pl.semaphore_wait(bar, 66)
 
     def make_gates():
@@ -194,21 +192,25 @@
             else:
                 copy(g * 8 + dz).start()
 
-    def c_start(g, carry):
-        start_group(c_copy, g)
-        return carry
-
-    def x_start(g, carry):
-        start_group(x_copy, g)
-        return carry
-
     own_c.start()
-    lax.fori_loop(0, 8, c_start, 0)
+    start_group(c_copy, 0)
+    start_group(c_copy, 1)
+
+    def c_start(dy, carry):
+        extract(craw, csend, dy)
+        start_group(c_copy, 2 * dy)
+        start_group(c_copy, 2 * dy + 1)
+        return carry
+
+    lax.fori_loop(1, 4, c_start, 0)
     loads[1].wait()
-    extract(xraw, xsend)
+
+    def x_ready(dy, carry):
+        extract(xraw, xsend, dy)
+        return carry
+
+    lax.fori_loop(0, 4, x_ready, 0)
     own_x.start()
-    if X_LAG < 0:
-        lax.fori_loop(0, 8, x_start, 0)
     loads[2].wait()
     make_gates()
 
@@ -250,10 +252,7 @@
         near(g, 0).start()
         near(g, 1).start()
 
-        if X_LAG >= 0:
-            @pl.when(g >= X_LAG)
-            def _():
-                start_group(x_copy, g - X_LAG)
+        start_group(x_copy, g)
 
         @pl.when(g >= 1)
         def _():
@@ -262,8 +261,6 @@
         return carry
 
     lax.fori_loop(0, 8, arrive, 0)
-    if X_LAG > 0:
-        lax.fori_loop(8 - X_LAG, 8, x_start, 0)
     relay(7)
 
     def all_n(m):
@@ -349,8 +346,6 @@
 
     turn_all(xq, xt, True)
     gate_one(xt, l1t, w1f, 0, 16)
-    gate_two(l1t, l2t, w2f, 0, 16)
-    turn_all(l2t, b2, False)
 
     def grad_two(i, acc):
         for u in range(8):
@@ -358,34 +353,40 @@
         return acc
 
     acc = lax.fori_loop(0, 4, grad_two, jnp.zeros((128, 256), F32))
-    e[256:384, :] = acc[:, :128]
-    e[384:512, :] = acc[:, 128:]
+    for k in range(NX):
+        e[k, 64:128, :] = acc[64 * (k % 2):64 * (k % 2) + 64, 128 * (k // 2):128 * (k // 2) + 128]
 
     def grad_one(i, acc):
         rows = pl.ds(8 * i, 8)
         return acc + dot_tn(b1t[rows].reshape(1024, 256), xt[rows].reshape(1024, 256))
 
     acc = lax.fori_loop(0, 4, grad_one, jnp.zeros((256, 256), F32))
-    e[0:128, :] = acc[0:128, 0:128] + acc[128:256, 128:256]
-    e[128:256, :] = acc[128:256, 0:128] - acc[0:128, 128:256]
+    for k in range(2):
+        i = slice(64 * k, 64 * k + 64)
+        j = slice(128 + 64 * k, 128 + 64 * k + 64)
+        e[k, 0:64, :] = acc[i, 0:128] + acc[j, 128:256]
+        e[2 + k, 0:64, :] = acc[j, 0:128] - acc[i, 128:256]
+
+    def one(dx):
+        to = (x + dx) % NX
+        return pltpu.make_async_remote_copy(
+            src_ref=e.at[to], dst_ref=rx.at[x],
+            send_sem=e1s.at[dx], recv_sem=e1r.at[dx], device_id=device(dx, 0, 0, 0), device_id_type=MESH)
+
+    for dx in range(1, NX):
+        one(dx).start()
+    rx[x] = e[x]
+
+    gate_two(l1t, l2t, w2f, 0, 16)
+    turn_all(l2t, b2, False)
 
     def grad_three(i, acc):
         for p in range(16):
             acc = acc + dot_nt(all_n(16 * i + p), with_turned(b2[16 * i + p]))
         return acc
 
-    acc3 = lax.fori_loop(0, 8, grad_three, jnp.zeros((128, 64), F32))
-    acc3 = jnp.transpose(jnp.concatenate([acc3, jnp.zeros((128, 64), F32)], axis=1))
-    e[512:768, :] = jnp.zeros((256, 128), F32)
-    spot = pl.multiple_of(32 * x, 32)
-    e[pl.ds(512 + spot, 32), :] = acc3[0:32, :]
-    e[pl.ds(640 + spot, 32), :] = acc3[32:64, :]
-
-    def one(dx):
-        to = (x + dx) % NX
-        return pltpu.make_async_remote_copy(
-            src_ref=e.at[pl.ds(pl.multiple_of(192 * to, 192), 192), :], dst_ref=rx.at[x],
-            send_sem=e1s.at[dx], recv_sem=e1r.at[dx], device_id=device(dx, 0, 0, 0), device_id_type=MESH)
+    acc = lax.fori_loop(0, 8, grad_three, jnp.zeros((128, 64), F32))
+    ryc[8, 128:192, :] = jnp.transpose(jnp.concatenate([acc, jnp.zeros((128, 64), F32)], axis=1))[0:64, :]
 
     def yc(k):
         return ((y + k // 2) % NY) * 2 + (c + k % 2) % NC
@@ -403,23 +404,20 @@
             send_sem=e3s.at[dz], recv_sem=e3r.at[dz], device_id=device(0, 0, dz, 0), device_id_type=MESH)
 
     def four(k):
-        rows = fin.at[pl.ds(pl.multiple_of(192 * x + 24 * (y * 2 + c), 8), 24), :]
+        rows = fin.at[x, pl.ds(pl.multiple_of(24 * (y * 2 + c), 8), 24), :]
         return pltpu.make_async_remote_copy(
             src_ref=rows, dst_ref=rows,
             send_sem=e4s.at[k], recv_sem=e4r.at[k], device_id=device(0, k // 2, 0, k % 2), device_id_type=MESH)
 
     def five(dx):
-        rows = fin.at[pl.ds(pl.multiple_of(192 * x, 192), 192), :]
+        rows = fin.at[x]
         return pltpu.make_async_remote_copy(
             src_ref=rows, dst_ref=rows,
             send_sem=e5s.at[dx], recv_sem=e5r.at[dx], device_id=device(dx, 0, 0, 0), device_id_type=MESH)
 
     for dx in range(1, NX):
-        one(dx).start()
-    rx[x] = e[pl.ds(pl.multiple_of(192 * x, 192), 192), :]
-    for dx in range(1, NX):
         one(dx).wait_recv()
-    ryc[8] = (rx[0] + rx[1]) + (rx[2] + rx[3])
+    ryc[8, 0:128, :] = (rx[0] + rx[1]) + (rx[2] + rx[3])
     for k in range(1, 8):
         two(k).start()
     ryc[y * 2 + c, 0:24, :] = ryc[8, pl.ds(pl.multiple_of(24 * (y * 2 + c), 8), 24), :]
@@ -439,7 +437,7 @@
     total = rz[0]
     for k in range(1, NZ):
         total = total + rz[k]
-    fin[pl.ds(pl.multiple_of(192 * x + 24 * (y * 2 + c), 8), 24), :] = total
+    fin[x, pl.ds(pl.multiple_of(24 * (y * 2 + c), 8), 24), :] = total
     for k in range(1, 8):
         four(k).start()
     for k in range(1, 8):
@@ -454,7 +452,13 @@
 
     factor = 1.0 / (128 * 64**0.5)
     sides = [(s, q) for s in range(3) for q in range(2)]
-    moved = [exact(pickers[s], fin[256 * s + 128 * q:256 * s + 128 * q + 128, :], ((0,), (1,) if s == 2 else (0,))) for s, q in sides]
+
+    def sums(s, q):
+        if s < 2:
+            return jnp.concatenate([fin[2 * q + k, 64 * s:64 * s + 64, :] for k in range(2)], axis=0)
+        return jnp.concatenate([fin[k, 128 + 32 * q:160 + 32 * q, :] for k in range(NX)], axis=0)
+
+    moved = [exact(pickers[s], sums(s, q), ((0,), (1,) if s == 2 else (0,))) for s, q in sides]
     for (s, q), part in zip(sides, moved):
         eout[s, q] = exact(part, pickers[s], ((1,), (0,))) * factor
 
@@ -492,22 +496,42 @@
             back(half, k).wait_send()
 
 
-def finish(sgr, sums, out, eout, outturn):
-    @pl.when(pl.program_id(0) == 0)
-    def _():
-        outturn[...] = output_turn()
-        eout[...] = sums[...]
-
-    made = []
-    for i in range(4):
-        n, rows = 2 * (i // 2), slice(64 * (i % 2), 64 * (i % 2) + 64)
-        sides = [jnp.concatenate([sgr[r, n + nn, rows, cc * 128:cc * 128 + 128] for r in range(2) for cc in range(2)], axis=0)
-                 for nn in range(2)]
-        made.append(dot(outturn[...], jnp.concatenate(sides, axis=1)).astype(BF))
-    for i in range(4):
-        n, at = 2 * (i // 2), slice(256 * (i % 2), 256 * (i % 2) + 256)
-        out[n, at, :] = made[i][:, :128]
-        out[n + 1, at, :] = made[i][:, 128:]
+def finish(back, sums, out, eout, outturn, sgr, given, held, in_s, out_s):
+    per = 16 // STEPS
+    come = pltpu.make_async_copy(sums, held, in_s.at[STEPS])
+    go = pltpu.make_async_copy(held, eout, out_s.at[STEPS])
+
+    def load(k):
+        at = pl.ds(per * k, per)
+        return pltpu.make_async_copy(back.at[:, at], sgr.at[:, at], in_s.at[k])
+
+    def give(k):
+        at = pl.ds(per * k, per)
+        return pltpu.make_async_copy(given.at[at], out.at[at], out_s.at[k])
+
+    for k in range(STEPS):
+        load(k).start()
+    come.start()
+    outturn[...] = output_turn()
+    for k in range(STEPS):
+        load(k).wait()
+        made = []
+        for i in range(per):
+            n, rows = per * k + 2 * (i // 2), slice(64 * (i % 2), 64 * (i % 2) + 64)
+            sides = [jnp.concatenate([sgr[r, n + nn, rows, cc * 128:cc * 128 + 128] for r in range(2) for cc in range(2)], axis=0)
+                     for nn in range(2)]
+            made.append(dot(outturn[...], jnp.concatenate(sides, axis=1)).astype(BF))
+        for i in range(per):
+            n, at = per * k + 2 * (i // 2), slice(256 * (i % 2), 256 * (i % 2) + 256)
+            given[n, at, :] = made[i][:, :128]
+            given[n + 1, at, :] = made[i][:, 128:]
+        give(k).start()
+        if k == 0:
+            come.wait()
+            go.start()
+    for k in range(STEPS):
+        give(k).wait()
+    go.wait()
 
 
 def local(initial_state, cotangent, gate_bank, slice_index, mode_order):
@@ -528,7 +552,7 @@
             big(64, 4, 16, 256), big(64, 4, 16, 256), big(8, 128, 16, 256), big(2, 128, 16, 256),
             big(128, 32, 256), big(32, 128, 256), big(32, 128, 256), big(32, 128, 256),
             big(32, 128, 256), big(32, 128, 256), big(32, 128, 256),
-            wide(768, 128), wide(4, 192, 128), wide(9, 192, 128), wide(8, 24, 128), wide(768, 128),
+            wide(4, 128, 128), wide(4, 128, 128), wide(9, 192, 128), wide(8, 24, 128), wide(4, 192, 128),
             sem(3), sem(64), sem(64), sem(64), sem(64), sem(2), sem(2, 8), sem(2, 8), sem(2, 8), sem(2, 8), sem(2, PIECES), sem(2, PIECES),
             sem(4), sem(4), sem(8), sem(8), sem(8), sem(8), sem(8), sem(8), sem(4), sem(4),
         ],
@@ -540,15 +564,11 @@
     )
     out, grads = pl.pallas_call(
         finish,
-        grid=(4,),
         out_shape=(jax.ShapeDtypeStruct((16, 512, 128), BF), jax.ShapeDtypeStruct((3, 2, 128, 128), F32)),
-        in_specs=[
-            pl.BlockSpec((2, 4, 128, 256), lambda i: (0, i, 0, 0)),
-            pl.BlockSpec((3, 2, 128, 128), lambda i: (0, 0, 0, 0)),
-        ],
-        out_specs=(pl.BlockSpec((4, 512, 128), lambda i: (i, 0, 0)), pl.BlockSpec((3, 2, 128, 128), lambda i: (0, 0, 0, 0))),
-        scratch_shapes=[big(256, 256)],
-        compiler_params=pltpu.CompilerParams(vmem_limit_bytes=FINISH_MIB << 20),
+        in_specs=[hbm, hbm],
+        out_specs=(hbm, hbm),
+        scratch_shapes=[big(256, 256), big(2, 16, 128, 256), big(16, 512, 128), wide(3, 2, 128, 128), sem(STEPS + 1), sem(STEPS + 1)],
+        compiler_params=pltpu.CompilerParams(vmem_limit_bytes=60 << 20),
         name="outputs",
     )(backs, sums)
     return grads, out.reshape(16, 128, 2, 2, 128)

time: 167 us -> 161 us (0.964)
  Pallas kernels: 166 us -> 160 us
    pallas_call x1, Pallas kernels: 161 us -> 157 us  [local(): pl.pallas_call(kernel, out_shape=(jax.ShapeDtypeStruct((2, 16, 128, 256),...]
where the time goes in v3:
time: 161 us
  Pallas kernels  160 us (99%)
    pallas_call x1, Pallas kernels, local(): pl.pallas_call(kernel, out_shape=(jax.ShapeDtypeStruct((2, 16, 128, 256),...  157 us

profile of v3, /device:TPU:1, one launch (start us, length us, event | category | flops | bytes accessed | tf_op | source)
XLA Modules:
  0.0 161.1 jit_solution(11055111484342210332)
XLA Ops:
  0.6 157.3 %gradients.1 = (bf16[2,16,128,256]{3,2,1,0:T(8,128)(2,1)}, f32[3,2,128,128]{3,2,1,0:T(8,128)}) custom-call(bf16[16,4,128,128]{3,2,1,0:T(8,128)(2,1)} %bitcast.3, bf16[16,4,128,128]{3,2,1,0:T(8,128)(2,1)} %bitcast.4, bf16[3,4,2,128,128]{4,3,2,1,0:T(8,128)(2,1)} %bank_in.1, s32[3]{0:T(128)} %slices.1, s32[3,7]{1,0:T(4,128)} %order.1), custom_call_target="tpu_custom_call" | custom-call | tf_op jit(solution)/shard_map/gradients/pallas_call | solution.py:544
  158.0 3.2 %outputs.1 = (bf16[16,512,128]{2,1,0:T(8,128)(2,1)}, f32[3,2,128,128]{3,2,1,0:T(8,128)}) custom-call(bf16[2,16,128,256]{3,2,1,0:T(8,128)(2,1)} %get-tuple-element.6.back, f32[3,2,128,128]{3,2,1,0:T(8,128)} %get-tuple-element.7.sums), custom_call_target="tpu_custom_call" | custom-call | tf_op jit(solution)/shard_map/outputs/pallas_call | solution.py:565

commit v4 on v3

--- a/solution.py
+++ b/solution.py
@@ -10,9 +10,12 @@
 F32 = jnp.float32
 HIGH = lax.Precision.HIGHEST
 NX, NY, NZ, NC = 4, 4, 8, 2
-Z_ORDER = (4, 3, 5, 2, 6, 1, 7, 0)
+Z_ORDER = (4, 3, 5, 2, 6, 1, 7)
+LAG = 3
 PIECES = 8
-EARLY = 5
+EARLY = 2
+PUMP = (2, 0, 1, 0, 2, 0, 1, 0)
+X_FIRST = 8
 STEPS = 2
 
 
@@ -85,8 +88,8 @@
     sgr, eout,
     craw, xraw, bank, pickers,
     w1f, w1b, w2f, w2b, w3b, w3all, turn,
-    csend, xsend, call, xq, b2, b2t, b1t, sg, xt, l1t, l2t, e, rx, ryc, rz, fin,
-    in_s, c_ss, c_rs, x_ss, x_rs, loc, g_ss, g_rs, f_ss, f_rs, s_ss, s_rs,
+    csend, xsend, cmid, xmid, call, xq, b2, b2t, b1t, sg, xt, l1t, l2t, e, rx, ryc, rz, fin,
+    in_s, cy_ss, cy_rs, xy_ss, xy_rs, c_ss, c_rs, x_ss, x_rs, c_own, x_own, g_ss, g_rs, f_ss, f_rs, s_ss, s_rs,
     e1s, e1r, e2s, e2r, e3s, e3r, e4s, e4r, e5s, e5r,
 ):
     grp, mem = lax.axis_index("grp"), lax.axis_index("mem")
@@ -98,20 +101,19 @@
         x2, y2, z2, c2 = (x + dx) % NX, (y + dy) % NY, (z + dz) % NZ, (c + dc) % NC
         return (x2 * 2 + z2 // 4, (y2 * 4 + z2 % 4) * 2 + c2)
 
-    def yzc(t):
-        return t // 16, t % 8, (t // 8) % 2
+    def group(q):
+        p = q // 2
+        return 2 * (p + (p // 2) * (1 - 2 * (p % 2))) + q % 2
 
     loads = [pltpu.make_async_copy(a, b, in_s.at[i]) for i, (a, b) in enumerate(((c_in, craw), (x_in, xraw), (bank_in, bank)))]
     for load in loads:
         load.start()
     bar = pltpu.get_barrier_semaphore()
 
-    def greet(t, carry):
-        dy, dz, dc = yzc(t)
-        pl.semaphore_signal(bar, inc=1, device_id=device(0, dy, dz, dc), device_id_type=MESH)
-        return carry
-
-    lax.fori_loop(1, 64, greet, 0)
+    for g in range(1, 8):
+        pl.semaphore_signal(bar, inc=1, device_id=device(0, g // 2, 0, g % 2), device_id_type=MESH)
+    for dz in range(1, NZ):
+        pl.semaphore_signal(bar, inc=1, device_id=device(0, 0, dz, 0), device_id_type=MESH)
     for dx in range(1, NX):
         pl.semaphore_signal(bar, inc=1, device_id=device(dx, 0, 0, 0), device_id_type=MESH)
 
@@ -123,17 +125,18 @@
             loaded.append(jnp.concatenate([raw[:, 2 * mp + mm, rows, :].reshape(256, 128) for mm in range(2)], axis=1))
         made = [dot(turn[...], v).astype(BF) for v in loaded]
         for i in range(4):
-            mp, r0 = i // 2, 8 * (first + i % 2)
+            mp = i // 2
             for mm in range(2):
                 for r in range(8):
+                    w = 8 * (i % 2) + r
                     for cc in range(2):
                         q = (r * 2 + cc) * 16
-                        send[r0 + r, 2 * mp + mm, :, cc * 128:cc * 128 + 128] = made[i][q:q + 16, mm * 128:mm * 128 + 128]
+                        send[(y + dy) % NY, w // 2 % 2, w // 4 + 4 * (w % 2), 2 * mp + mm, :, cc * 128:cc * 128 + 128] = made[i][q:q + 16, mm * 128:mm * 128 + 128]
 
     turn[...] = block_turn()
     loads[0].wait()
     extract(craw, csend, 0)
-    pl.semaphore_wait(bar, 66)
+    pl.semaphore_wait(bar, 17)
 
     def make_gates():
         for s in range(3):
@@ -158,65 +161,91 @@
         w3b[0:32, :] = w3all[pl.ds(at, 32), :]
         w3b[32:64, :] = w3all[pl.ds(128 + at, 32), :]
 
-    m_own = pl.multiple_of(y * 32 + c * 16 + zl * 4, 4)
-
-    def part_of(dy, dz, dc):
-        s = (z + dz + 6) % NZ
-        return 2 * ((((y + dy) % NY) * 4 + s % 4) * 2 + (c + dc) % NC) + s // 4
-
-    def c_copy(t):
-        dy, dz, dc = yzc(t)
-        return pltpu.make_async_remote_copy(
-            src_ref=csend.at[part_of(dy, dz, dc)],
-            dst_ref=call.at[grp, pl.ds(m_own, 4)],
-            send_sem=c_ss.at[t], recv_sem=c_rs.at[t],
-            device_id=device(0, dy, dz, dc), device_id_type=MESH)
-
-    def x_copy(t):
-        dy, dz, dc = yzc(t)
-        return pltpu.make_async_remote_copy(
-            src_ref=xsend.at[part_of(dy, dz, dc)],
-            dst_ref=xq.at[zh, pl.ds(m_own, 4)],
-            send_sem=x_ss.at[t], recv_sem=x_rs.at[t],
-            device_id=device(0, dy, dz, dc), device_id_type=MESH)
-
-    own_c = pltpu.make_async_copy(csend.at[part_of(0, 0, 0)], call.at[grp, pl.ds(m_own, 4)], loc.at[0])
-    own_x = pltpu.make_async_copy(xsend.at[part_of(0, 0, 0)], xq.at[zh, pl.ds(m_own, 4)], loc.at[1])
-
-    def start_group(copy, g):
-        for dz in Z_ORDER:
-            if dz == 0:
-                @pl.when(g > 0)
-                def _():
-                    copy(g * 8).start()
-            else:
-                copy(g * 8 + dz).start()
-
-    own_c.start()
-    start_group(c_copy, 0)
-    start_group(c_copy, 1)
-
-    def c_start(dy, carry):
-        extract(craw, csend, dy)
-        start_group(c_copy, 2 * dy)
-        start_group(c_copy, 2 * dy + 1)
-        return carry
-
-    lax.fori_loop(1, 4, c_start, 0)
-    loads[1].wait()
-
-    def x_ready(dy, carry):
-        extract(xraw, xsend, dy)
-        return carry
-
-    lax.fori_loop(0, 4, x_ready, 0)
-    own_x.start()
-    loads[2].wait()
-    make_gates()
-
     def m_of(g):
         dy, dc = g // 2, g % 2
         return pl.multiple_of(((y + NY - dy) % NY) * 32 + ((c + NC - dc) % NC) * 16, 16)
+
+    def place(dz):
+        return (z + dz + 6) % NZ
+
+    def mover(send, mid, land, spot, y_ss, y_rs, z_ss, z_rs, own_s):
+        def over_y(g):
+            dy, dc = g // 2, g % 2
+            return pltpu.make_async_remote_copy(
+                src_ref=send.at[(y + dy) % NY, (c + dc) % NC], dst_ref=mid.at[g],
+                send_sem=y_ss.at[g], recv_sem=y_rs.at[g], device_id=device(0, dy, 0, dc), device_id_type=MESH)
+
+        def source(g, dz, own):
+            return send.at[y, c, place(dz)] if own else mid.at[g, place(dz)]
+
+        def target(g):
+            return land.at[spot, pl.ds(pl.multiple_of(m_of(g) + 4 * zl, 4), 4)]
+
+        def over_z(g, dz, own=False):
+            return pltpu.make_async_remote_copy(
+                src_ref=source(g, dz, own), dst_ref=target(g), send_sem=z_ss.at[g, dz], recv_sem=z_rs.at[g, dz],
+                device_id=device(0, 0, dz, 0), device_id_type=MESH)
+
+        def stay(g, own=False):
+            return pltpu.make_async_copy(source(g, 0, own), target(g), own_s.at[g])
+
+        def go(g, own=False):
+            for dz in Z_ORDER:
+                over_z(g, dz, own).start()
+            stay(g, own).start()
+
+        def pass_on(g):
+            over_y(g).wait_recv()
+            go(g)
+
+        def come(g):
+            for dz in Z_ORDER:
+                over_z(g, dz).wait_recv()
+            stay(g).wait()
+
+        def gone():
+            def body(g, carry):
+                @pl.when(g > 0)
+                def _():
+                    over_y(g).wait_send()
+
+                for dz in Z_ORDER:
+                    over_z(g, dz).wait_send()
+                return carry
+
+            lax.fori_loop(0, 8, body, 0)
+
+        return over_y, go, pass_on, come, gone
+
+    c_over_y, c_go, c_pass_on, c_come, c_gone = mover(csend, cmid, call, grp, cy_ss, cy_rs, c_ss, c_rs, c_own)
+    x_over_y, x_go, x_pass_on, x_come, x_gone = mover(xsend, xmid, xq, zh, xy_ss, xy_rs, x_ss, x_rs, x_own)
+
+    c_go(0, True)
+    c_over_y(1).start()
+
+    def c_start(p, carry):
+        g = group(2 * p)
+        extract(craw, csend, g // 2)
+        c_over_y(g).start()
+        c_over_y(g + 1).start()
+        return carry
+
+    lax.fori_loop(1, 4, c_start, 0)
+    c_pass_on(1)
+    loads[1].wait()
+
+    def x_start(p, carry):
+        g = group(2 * p)
+        extract(xraw, xsend, g // 2)
+
+        @pl.when(p > 0)
+        def _():
+            x_over_y(g).start()
+
+        x_over_y(g + 1).start()
+        return carry
+
+    lax.fori_loop(0, 4, x_start, 0)
 
     def near(g, way):
         part = call.at[pl.ds(2 * x, 2), pl.ds(m_of(g), 16)]
@@ -236,37 +265,46 @@
             near(g, way).wait_recv()
             far(g, way).start()
 
-    def arrive(g, carry):
-        for dz in Z_ORDER:
-            if dz == 0:
-                @pl.when(g > 0)
-                def _():
-                    c_copy(g * 8).wait_recv()
-            else:
-                c_copy(g * 8 + dz).wait_recv()
-
-        @pl.when(g == 0)
-        def _():
-            own_c.wait()
-
+    def arrive(h):
+        g = group(h)
+        c_come(g)
         near(g, 0).start()
         near(g, 1).start()
 
-        start_group(x_copy, g)
-
-        @pl.when(g >= 1)
+    def early(q, carry):
+        c_pass_on(group(q))
+
+        @pl.when(q >= LAG)
         def _():
-            relay(g - 1)
-
-        return carry
-
-    lax.fori_loop(0, 8, arrive, 0)
-    relay(7)
+            arrive(q - LAG)
+
+        @pl.when(q > LAG)
+        def _():
+            relay(group(q - LAG - 1))
+
+        return carry
+
+    lax.fori_loop(2, 8, early, 0)
+    loads[2].wait()
+    make_gates()
+    x_go(0, True)
+    x_pass_on(1)
+
+    def late(h, carry):
+        arrive(h)
+        relay(group(h - 1))
+        x_pass_on(group(2 * (h + LAG - 7)))
+        x_pass_on(group(2 * (h + LAG - 7) + 1))
+        return carry
+
+    lax.fori_loop(8 - LAG, 8, late, 0)
+    relay(group(7))
 
     def all_n(m):
         return call[:, m].reshape(128, 256)
 
-    def third(g, carry):
+    def third(h, carry):
+        g = group(h)
         far(g, 0).wait_recv()
         far(g, 1).wait_recv()
 
@@ -332,18 +370,22 @@
             n = 16 * half + 8 * k
             gate_two(b2t, b1t, w2b, n, 4)
             gate_one(b1t, sg, w1b, n, 4)
-        for j in range(PIECES // 2 * k, PIECES // 2 * (k + 1)):
-            if j < EARLY:
-                back(0, j).start()
-                back(1, j).start()
-
-    def x_arrive(t, carry):
-        x_copy(t).wait_recv()
-        return carry
-
-    own_x.wait()
-    lax.fori_loop(1, 64, x_arrive, 0)
-
+
+    def pump(stop):
+        first = EARLY + sum(PUMP[:stop])
+        for j in range(first, PIECES if stop == len(PUMP) - 1 else first + PUMP[stop]):
+            back(0, j).start()
+            back(1, j).start()
+
+    def x_arrive(h, carry):
+        x_come(group(h))
+        return carry
+
+    lax.fori_loop(0, X_FIRST, x_arrive, 0)
+    for j in range(EARLY):
+        back(0, j).start()
+        back(1, j).start()
+    lax.fori_loop(X_FIRST, 8, x_arrive, 0)
     turn_all(xq, xt, True)
     gate_one(xt, l1t, w1f, 0, 16)
 
@@ -377,6 +419,7 @@
         one(dx).start()
     rx[x] = e[x]
 
+    pump(0)
     gate_two(l1t, l2t, w2f, 0, 16)
     turn_all(l2t, b2, False)
 
@@ -415,35 +458,39 @@
             src_ref=rows, dst_ref=rows,
             send_sem=e5s.at[dx], recv_sem=e5r.at[dx], device_id=device(dx, 0, 0, 0), device_id_type=MESH)
 
+    pump(1)
     for dx in range(1, NX):
         one(dx).wait_recv()
     ryc[8, 0:128, :] = (rx[0] + rx[1]) + (rx[2] + rx[3])
     for k in range(1, 8):
         two(k).start()
     ryc[y * 2 + c, 0:24, :] = ryc[8, pl.ds(pl.multiple_of(24 * (y * 2 + c), 8), 24), :]
+    pump(2)
     for k in range(1, 8):
         two(k).wait_recv()
+    pump(3)
     total = ryc[0, 0:24, :]
     for k in range(1, 8):
         total = total + ryc[k, 0:24, :]
     rz[z] = total
     for dz in range(1, NZ):
         three(dz).start()
-    for j in range(EARLY, PIECES):
-        back(0, j).start()
-        back(1, j).start()
+    pump(4)
     for dz in range(1, NZ):
         three(dz).wait_recv()
+    pump(5)
     total = rz[0]
     for k in range(1, NZ):
         total = total + rz[k]
     fin[x, pl.ds(pl.multiple_of(24 * (y * 2 + c), 8), 24), :] = total
     for k in range(1, 8):
         four(k).start()
+    pump(6)
     for k in range(1, 8):
         four(k).wait_recv()
     for dx in range(1, NX):
         five(dx).start()
+    pump(7)
     for dx in range(1, NX):
         five(dx).wait_recv()
 
@@ -462,12 +509,8 @@
     for (s, q), part in zip(sides, moved):
         eout[s, q] = exact(part, pickers[s], ((1,), (0,))) * factor
 
-    def c_gone(t, carry):
-        c_copy(t).wait_send()
-        x_copy(t).wait_send()
-        return carry
-
-    lax.fori_loop(1, 64, c_gone, 0)
+    c_gone()
+    x_gone()
 
     def g_gone(g, carry):
         for way in range(2):
@@ -549,11 +592,11 @@
         scratch_shapes=[
             big(16, 4, 128, 128), big(16, 4, 128, 128), big(3, 4, 2, 128, 128), wide(3, 128, 128),
             big(256, 256), big(256, 256), big(256, 256), big(256, 256), big(64, 256), big(256, 256), big(256, 256),
-            big(64, 4, 16, 256), big(64, 4, 16, 256), big(8, 128, 16, 256), big(2, 128, 16, 256),
+            big(4, 2, 8, 4, 16, 256), big(4, 2, 8, 4, 16, 256), big(8, 8, 4, 16, 256), big(8, 8, 4, 16, 256), big(8, 128, 16, 256), big(2, 128, 16, 256),
             big(128, 32, 256), big(32, 128, 256), big(32, 128, 256), big(32, 128, 256),
             big(32, 128, 256), big(32, 128, 256), big(32, 128, 256),
             wide(4, 128, 128), wide(4, 128, 128), wide(9, 192, 128), wide(8, 24, 128), wide(4, 192, 128),
-            sem(3), sem(64), sem(64), sem(64), sem(64), sem(2), sem(2, 8), sem(2, 8), sem(2, 8), sem(2, 8), sem(2, PIECES), sem(2, PIECES),
+            sem(3), sem(8), sem(8), sem(8), sem(8), sem(8, 8), sem(8, 8), sem(8, 8), sem(8, 8), sem(8), sem(8), sem(2, 8), sem(2, 8), sem(2, 8), sem(2, 8), sem(2, PIECES), sem(2, PIECES),
             sem(4), sem(4), sem(8), sem(8), sem(8), sem(8), sem(8), sem(8), sem(4), sem(4),
         ],
         compiler_params=pltpu.CompilerParams(collective_id=0, has_side_effects=True, vmem_limit_bytes=54 << 20),

time: 161 us -> 161 us (level)
  no operation moved by 1% of the time
where the time goes in v4:
time: 161 us; the launch traced here: 160 us
  Pallas kernels  160 us (99%)
    pallas_call x1, Pallas kernels, local(): pl.pallas_call(kernel, out_shape=(jax.ShapeDtypeStruct((2, 16, 128, 256),...  157 us

profile of v4, /device:TPU:1, one launch (start us, length us, event | category | flops | bytes accessed | tf_op | source)
XLA Modules:
  0.0 160.5 jit_solution(14406572891219081962)
XLA Ops:
  0.6 156.7 %gradients.1 = (bf16[2,16,128,256]{3,2,1,0:T(8,128)(2,1)}, f32[3,2,128,128]{3,2,1,0:T(8,128)}) custom-call(bf16[16,4,128,128]{3,2,1,0:T(8,128)(2,1)} %bitcast.3, bf16[16,4,128,128]{3,2,1,0:T(8,128)(2,1)} %bitcast.4, bf16[3,4,2,128,128]{4,3,2,1,0:T(8,128)(2,1)} %bank_in.1, s32[3]{0:T(128)} %slices.1, s32[3,7]{1,0:T(4,128)} %order.1), custom_call_target="tpu_custom_call" | custom-call | tf_op jit(solution)/shard_map/gradients/pallas_call | solution.py:587
  157.3 3.2 %outputs.1 = (bf16[16,512,128]{2,1,0:T(8,128)(2,1)}, f32[3,2,128,128]{3,2,1,0:T(8,128)}) custom-call(bf16[2,16,128,256]{3,2,1,0:T(8,128)(2,1)} %get-tuple-element.6.back, f32[3,2,128,128]{3,2,1,0:T(8,128)} %get-tuple-element.7.sums), custom_call_target="tpu_custom_call" | custom-call | tf_op jit(solution)/shard_map/outputs/pallas_call | solution.py:608

commit v5 on v4

--- a/solution.py
+++ b/solution.py
@@ -13,9 +13,9 @@
 Z_ORDER = (4, 3, 5, 2, 6, 1, 7)
 LAG = 3
 PIECES = 8
-EARLY = 2
-PUMP = (2, 0, 1, 0, 2, 0, 1, 0)
-X_FIRST = 8
+EARLY = 1
+PUMP = (2, 0, 1, 0, 2, 0, 1, 1)
+X_FIRST = 6
 STEPS = 2
 
 
@@ -88,7 +88,7 @@
     sgr, eout,
     craw, xraw, bank, pickers,
     w1f, w1b, w2f, w2b, w3b, w3all, turn,
-    csend, xsend, cmid, xmid, call, xq, b2, b2t, b1t, sg, xt, l1t, l2t, e, rx, ryc, rz, fin,
+    csend, xsend, cmid, xmid, call, xq, b2, b2t, b1t, sg, l1t, l2t, e, rx, ryc, rz, fin,
     in_s, cy_ss, cy_rs, xy_ss, xy_rs, c_ss, c_rs, x_ss, x_rs, c_own, x_own, g_ss, g_rs, f_ss, f_rs, s_ss, s_rs,
     e1s, e1r, e2s, e2r, e3s, e3r, e4s, e4r, e5s, e5r,
 ):
@@ -377,17 +377,25 @@
             back(0, j).start()
             back(1, j).start()
 
-    def x_arrive(h, carry):
-        x_come(group(h))
-        return carry
-
-    lax.fori_loop(0, X_FIRST, x_arrive, 0)
+    def x_arrive(h, acc):
+        g = group(h)
+        x_come(g)
+        m = pl.ds(m_of(g), 16)
+        rows = [dot(turn[...], xq[nb, m].reshape(256, 256)).astype(BF) for nb in range(2)]
+        rows = jnp.concatenate(rows, axis=0)
+        l1t[:, m, :] = dot(rows, w1f[...]).astype(BF).reshape(32, 16, 256)
+        return acc + dot_tn(b1t[:, m, :].reshape(512, 256), rows)
+
+    v1 = lax.fori_loop(0, X_FIRST, x_arrive, jnp.zeros((256, 256), F32))
     for j in range(EARLY):
         back(0, j).start()
         back(1, j).start()
-    lax.fori_loop(X_FIRST, 8, x_arrive, 0)
-    turn_all(xq, xt, True)
-    gate_one(xt, l1t, w1f, 0, 16)
+    v1 = lax.fori_loop(X_FIRST, 8, x_arrive, v1)
+    for k in range(2):
+        i = slice(64 * k, 64 * k + 64)
+        j = slice(128 + 64 * k, 128 + 64 * k + 64)
+        e[k, 0:64, :] = v1[i, 0:128] + v1[j, 128:256]
+        e[2 + k, 0:64, :] = v1[j, 0:128] - v1[i, 128:256]
 
     def grad_two(i, acc):
         for u in range(8):
@@ -398,17 +406,6 @@
     for k in range(NX):
         e[k, 64:128, :] = acc[64 * (k % 2):64 * (k % 2) + 64, 128 * (k // 2):128 * (k // 2) + 128]
 
-    def grad_one(i, acc):
-        rows = pl.ds(8 * i, 8)
-        return acc + dot_tn(b1t[rows].reshape(1024, 256), xt[rows].reshape(1024, 256))
-
-    acc = lax.fori_loop(0, 4, grad_one, jnp.zeros((256, 256), F32))
-    for k in range(2):
-        i = slice(64 * k, 64 * k + 64)
-        j = slice(128 + 64 * k, 128 + 64 * k + 64)
-        e[k, 0:64, :] = acc[i, 0:128] + acc[j, 128:256]
-        e[2 + k, 0:64, :] = acc[j, 0:128] - acc[i, 128:256]
-
     def one(dx):
         to = (x + dx) % NX
         return pltpu.make_async_remote_copy(
@@ -424,11 +421,11 @@
     turn_all(l2t, b2, False)
 
     def grad_three(i, acc):
-        for p in range(16):
-            acc = acc + dot_nt(all_n(16 * i + p), with_turned(b2[16 * i + p]))
+        for p in range(32):
+            acc = acc + dot_nt(all_n(32 * i + p), with_turned(b2[32 * i + p]))
         return acc
 
-    acc = lax.fori_loop(0, 8, grad_three, jnp.zeros((128, 64), F32))
+    acc = lax.fori_loop(0, 4, grad_three, jnp.zeros((128, 64), F32))
     ryc[8, 128:192, :] = jnp.transpose(jnp.concatenate([acc, jnp.zeros((128, 64), F32)], axis=1))[0:64, :]
 
     def yc(k):
@@ -594,7 +591,7 @@
             big(256, 256), big(256, 256), big(256, 256), big(256, 256), big(64, 256), big(256, 256), big(256, 256),
             big(4, 2, 8, 4, 16, 256), big(4, 2, 8, 4, 16, 256), big(8, 8, 4, 16, 256), big(8, 8, 4, 16, 256), big(8, 128, 16, 256), big(2, 128, 16, 256),
             big(128, 32, 256), big(32, 128, 256), big(32, 128, 256), big(32, 128, 256),
-            big(32, 128, 256), big(32, 128, 256), big(32, 128, 256),
+            big(32, 128, 256), big(32, 128, 256),
             wide(4, 128, 128), wide(4, 128, 128), wide(9, 192, 128), wide(8, 24, 128), wide(4, 192, 128),
             sem(3), sem(8), sem(8), sem(8), sem(8), sem(8, 8), sem(8, 8), sem(8, 8), sem(8, 8), sem(8), sem(8), sem(2, 8), sem(2, 8), sem(2, 8), sem(2, 8), sem(2, PIECES), sem(2, PIECES),
             sem(4), sem(4), sem(8), sem(8), sem(8), sem(8), sem(8), sem(8), sem(4), sem(4),

time: 161 us -> 160 us (level)
  Pallas kernels: 160 us -> 158 us
    pallas_call x1, Pallas kernels: 157 us -> 155 us  [local(): pl.pallas_call(kernel, out_shape=(jax.ShapeDtypeStruct((2, 16, 128, 256),...]
where the time goes in v5:
time: 160 us; the launch traced here: 158 us
  Pallas kernels  158 us (99%)
    pallas_call x1, Pallas kernels, local(): pl.pallas_call(kernel, out_shape=(jax.ShapeDtypeStruct((2, 16, 128, 256),...  155 us

profile of v5, /device:TPU:1, one launch (start us, length us, event | category | flops | bytes accessed | tf_op | source)
XLA Modules:
  0.0 158.5 jit_solution(10844736198205256012)
XLA Ops:
  0.6 154.7 %gradients.1 = (bf16[2,16,128,256]{3,2,1,0:T(8,128)(2,1)}, f32[3,2,128,128]{3,2,1,0:T(8,128)}) custom-call(bf16[16,4,128,128]{3,2,1,0:T(8,128)(2,1)} %bitcast.3, bf16[16,4,128,128]{3,2,1,0:T(8,128)(2,1)} %bitcast.4, bf16[3,4,2,128,128]{4,3,2,1,0:T(8,128)(2,1)} %bank_in.1, s32[3]{0:T(128)} %slices.1, s32[3,7]{1,0:T(4,128)} %order.1), custom_call_target="tpu_custom_call" | custom-call | tf_op jit(solution)/shard_map/gradients/pallas_call | solution.py:584
  155.3 3.2 %outputs.1 = (bf16[16,512,128]{2,1,0:T(8,128)(2,1)}, f32[3,2,128,128]{3,2,1,0:T(8,128)}) custom-call(bf16[2,16,128,256]{3,2,1,0:T(8,128)(2,1)} %get-tuple-element.6.back, f32[3,2,128,128]{3,2,1,0:T(8,128)} %get-tuple-element.7.sums), custom_call_target="tpu_custom_call" | custom-call | tf_op jit(solution)/shard_map/outputs/pallas_call | solution.py:605
